TPU v7x, 32 devices: a whole 2x2x4 slice. The times are simulated.
32 devices in a mesh: dom: 4 (over x, core), tile: 8 (over z, y).
Axes of the slice: x: 2, y: 2, z: 4, core: 2. Of those that a mesh axis runs over, the one named last changes fastest.
Arguments:
- embedding: bfloat16 [8192, 1152], P(('dom', 'tile')), may hold values from -6 to 6
- ghost_index: int32 [8192], P(('dom', 'tile')), may hold values from 0 to 255
- tile_count: int32 [4, 8], P('dom'), may hold values from 1 to 96, 384 in all within a row
- edge_source: int32 [393216], P(('dom', 'tile')), may hold values from 0 to 4095
- edge_target: int32 [393216], P(('dom', 'tile')), may hold values from 0 to 255
- edge_features: bfloat16 [393216, 128], P(('dom', 'tile')), may hold values from -6 to 6
- radial_in: bfloat16 [128, 128], replicated, may hold values from -0.5 to 0.5
- radial_out: bfloat16 [128, 384], replicated, may hold values from -0.5 to 0.5
- mix_weight: bfloat16 [3, 256, 128], replicated, may hold values from -0.375 to 0.375
Outputs:
- update: bfloat16 [8192, 1152], P(('dom', 'tile'))
Inputs may be any that keep to these rules, and one draw needn't show every extreme that they name: `tile_count`: each row of 8 counts sums to 384 and its largest equals 96.
All inputs are finite; a program needn't handle non-finite values.
Results may differ from a plain program's by a relative error of at most 0.0044.
Values may be sent and summed in bfloat16 or wider, within the bound.
No kernel may reach another device: no remote copies, remote signals or barrier semaphores. Data moves between devices by JAX's collectives and lax.ppermute only.
A program may use at most 128 MiB of HBM per device.

v0:
```python
import functools
import jax
import jax.numpy as jnp
from jax import lax
from jax.experimental import pallas as pl
from jax.experimental.pallas import tpu as pltpu
from jax.sharding import PartitionSpec as P

C = 128
K = 9
ATOM_DEV = 256
GHOST = 128
TE = 128
BE = 256
CHUNK = 256
CHUNK_BITS = 8
WIDTH = K * C
EXTRA = 16
PER = 4
degree_of = (0, 1, 1, 1, 2, 2, 2, 2, 2)
inv_scale = 0.125

F32 = jnp.float32
BF16 = jnp.bfloat16
I32 = jnp.int32

PARAMS = pltpu.CompilerParams(vmem_limit_bytes=58 * 1024 * 1024)


def vmem():
    return pl.BlockSpec(memory_space=pltpu.VMEM)


def smem():
    return pl.BlockSpec(memory_space=pltpu.SMEM)


def cols(k):
    return slice(k * C, (k + 1) * C)


def iota(shape, dim):
    return lax.broadcasted_iota(I32, shape, dim)


def as_bf16(mask):
    return jnp.where(mask, 1.0, 0.0).astype(BF16)


def dot(a, b):
    return jnp.dot(a, b, preferred_element_type=F32)


def mix_kernel(x_ref, mix_ref, pick_ref, mixed_ref):
    for k in range(K):
        mixed = dot(x_ref[:, cols(k)], mix_ref[degree_of[k], :C])
        mixed_ref[cols(k), :] = mixed.T.astype(BF16)
    picks = jnp.broadcast_to(pick_ref[...].astype(F32), (EXTRA, ATOM_DEV))
    mixed_ref[WIDTH:, :] = picks.astype(BF16)


def pick_kernel(*refs):
    *blocks, down_ref, up_ref = refs
    for i, rows_ref in enumerate(blocks):
        picks = rows_ref[WIDTH:, :].astype(F32)[:1, :].astype(I32)
        chosen = as_bf16(iota((ATOM_DEV, 2 * GHOST), 0) == picks)
        rows = dot(rows_ref[:WIDTH, :], chosen).astype(BF16)
        down_ref[i] = rows[:, :GHOST]
        up_ref[i] = rows[:, GHOST:]


def rank_kernel(count_ref, src_ref, label_ref, pos_ref, span_ref, oh_ref, cum_ref, *, slots):
    tiles = src_ref.shape[0]
    nb = span_ref.shape[0] // 3
    count = count_ref[0]
    label = label_ref[...]

    def mark(t, carry):
        bucket = src_ref[pl.ds(t, 1), :] >> CHUNK_BITS
        bucket = jnp.where(t < count, bucket, -1)
        oh_ref[pl.ds(pl.multiple_of(t * nb, nb), nb), :] = as_bf16(label == bucket)
        return carry

    lax.fori_loop(0, tiles, mark, 0, unroll=8)
    upto = as_bf16(iota((TE, TE), 0) <= iota((TE, TE), 1))
    both = jnp.concatenate([upto, jnp.ones((TE, TE), BF16)], axis=1)
    step = 256
    for r in range(0, tiles * nb, step):
        cum_ref[r : r + step, :] = dot(oh_ref[r : r + step, :], both)

    def add(t, total):
        return total + cum_ref[pl.ds(pl.multiple_of(t * nb, nb), nb), TE:]

    total = lax.fori_loop(0, tiles, add, jnp.zeros((nb, TE), F32), unroll=8)
    blocks = jnp.floor((total + (BE - 1)) * (1.0 / BE))
    below = as_bf16(iota((nb, nb), 1) < iota((nb, nb), 0))
    first = dot(below, blocks.astype(BF16))
    span_ref[:nb, :] = first.astype(I32)
    span_ref[nb : 2 * nb, :] = blocks.astype(I32)
    passed = jnp.where(iota((nb, TE), 1).astype(F32) >= first + blocks, 1.0, 0.0)
    chunk_of = jnp.minimum(jnp.sum(passed, axis=0, keepdims=True), nb - 1.0)
    span_ref[2 * nb :, :] = jnp.broadcast_to(chunk_of, (nb, TE)).astype(I32)

    def place(t, run):
        rows = pl.ds(pl.multiple_of(t * nb, nb), nb)
        oh = oh_ref[rows, :].astype(F32)
        value = oh * (cum_ref[rows, :TE] + run)
        place_of = jnp.sum(value, axis=0, keepdims=True).astype(I32)
        pos_ref[pl.ds(t, 1), :] = jnp.where(t < count, 2 * place_of, 2 * slots)
        return run + cum_ref[rows, TE:]

    lax.fori_loop(0, tiles, place, first * BE - 1.0, unroll=8)


def radial_kernel(count_ref, tgt_ref, feat_ref, rin_ref, rad_ref, rsum_ref):
    tiles = tgt_ref.shape[0]
    count = count_ref[0]
    rsum_ref[...] = jnp.zeros_like(rsum_ref)
    group = 4
    atom_id = iota((ATOM_DEV, TE), 0)

    def step(i, carry):
        rows = pl.ds(pl.multiple_of(i * (group * TE), group * TE), group * TE)
        hidden = dot(feat_ref[rows, :], rin_ref[...])
        radial = (hidden / (1.0 + jnp.exp(-hidden))).astype(BF16)
        rad_ref[rows, :] = radial
        land = []
        for q in range(group):
            t = i * group + q
            tgt = jnp.where(t < count, tgt_ref[pl.ds(t, 1), :], -1)
            land.append(as_bf16(atom_id == tgt))
        rsum_ref[...] += dot(jnp.concatenate(land, axis=1), radial)
        return carry

    lax.fori_loop(0, (count + group - 1) // group, step, 0)


def place_kernel(
    count_ref, pos_ref, span_ref, src_ref, tgt_ref, rin_ref, rad_ref, tgtb_ref, srcs_ref, pairs, even, odd
):
    tiles = src_ref.shape[0]
    nb = span_ref.shape[0] // 3
    count = count_ref[0]
    blank = jnp.where((iota((2 * BE, C), 0) & 1) == 1, -1.0, 0.0)

    def clear(b, carry):
        blocks = span_ref[nb + b, 0]

        @pl.when(blocks > 0)
        def _():
            last = pl.multiple_of((span_ref[b, 0] + blocks - 1) * (2 * BE), 2 * BE)
            pairs[pl.ds(last, 2 * BE), :] = blank

        return carry

    lax.fori_loop(0, nb, clear, 0)
    eye = iota((TE, TE), 0) == iota((TE, TE), 1)
    spread = jnp.concatenate(
        [jnp.ones((TE, C), BF16), jnp.full((TE, C), float(CHUNK), BF16)], axis=0
    )

    def compute(t, out):
        t = jnp.minimum(t, tiles - 1)
        rows = pl.ds(pl.multiple_of(t * TE, TE), TE)
        out[pl.ds(0, TE, stride=2), :] = rin_ref[rows, :].astype(F32)
        src = src_ref[pl.ds(t, 1), :] & (CHUNK - 1)
        tgt = tgt_ref[pl.ds(t, 1), :]
        diag_s = jnp.where(eye, src.astype(F32), 0.0).astype(BF16)
        diag_t = jnp.where(eye, tgt.astype(F32), 0.0).astype(BF16)
        code = dot(jnp.concatenate([diag_s, diag_t], axis=1), spread)
        out[pl.ds(1, TE, stride=2), :] = code

    def scatter(t, data):
        for e in range(TE):
            pairs[pl.ds(pos_ref[t, e], 2), :] = data[2 * e : 2 * e + 2, :]

    compute(0, even)

    def step(i, carry):
        compute(2 * i + 1, odd)
        scatter(2 * i, even)
        compute(2 * i + 2, even)
        scatter(2 * i + 1, odd)
        return carry

    lax.fori_loop(0, (count + 1) // 2, step, 0)

    def finish(j, carry):
        rows = pl.ds(pl.multiple_of(j * BE, BE), BE)
        base = pl.multiple_of(j * (2 * BE), 2 * BE)
        rad_ref[rows, :] = pairs[pl.ds(base, BE, stride=2), :].astype(BF16)
        code = pairs[pl.ds(base + 1, BE, stride=2), :].astype(I32)
        tgtb_ref[rows, :] = (code >> CHUNK_BITS).astype(F32).astype(BF16)
        src = (code & (CHUNK - 1)).astype(F32)
        for h in range(BE // TE):
            part = jnp.where(eye, src[h * TE : (h + 1) * TE, :], 0.0)
            row = pl.ds(j * (BE // TE) + h, 1)
            srcs_ref[row, :] = jnp.sum(part, axis=0, keepdims=True).astype(I32)
        return carry

    used = span_ref[nb - 1, 0] + span_ref[2 * nb - 1, 0]
    lax.fori_loop(0, used, finish, 0)


def main_kernel(*refs, low, n_ghost, n_own, first, final):
    span_ref, *refs = refs
    ghosts, refs = refs[: 2 * (n_ghost > 0)], refs[2 * (n_ghost > 0) :]
    owns, refs = refs[:n_own], refs[n_own:]
    rad_hbm, tgt_hbm, src_ref, rout_ref, *refs = refs
    if not first:
        part_ref, *refs = refs
    if final:
        rsum_ref, x_ref, mix_ref, *refs = refs
    out_ref, rbuf, tbuf, land_ref, message_ref, tables, sems, table_sems, *refs = refs
    acc_ref = refs[0] if final else out_ref
    count = n_ghost + n_own
    nb = span_ref.shape[0] // 3
    begin = span_ref[low, 0]
    end = span_ref[low + count - 1, 0] + span_ref[nb + low + count - 1, 0]
    groups = (end - begin + PER - 1) // PER

    loads = []
    for i, own in enumerate(owns):
        loads.append((own.at[:WIDTH, :], tables.at[n_ghost + i]))
    for i in range(n_ghost):
        for side in range(2):
            half = tables.at[i, :, side * GHOST : (side + 1) * GHOST]
            loads.append((ghosts[side].at[i], half))
    loads = [
        pltpu.make_async_copy(src, dst, table_sems.at[i]) for i, (src, dst) in enumerate(loads)
    ]
    for load in loads:
        load.start()

    def copies(p, slot):
        moves = []
        for h in range(PER):
            j = jnp.minimum(begin + PER * p + h, end - 1)
            rows = pl.ds(pl.multiple_of(j * BE, BE), BE)
            moves.append(
                pltpu.make_async_copy(rad_hbm.at[rows, :], rbuf.at[slot, h], sems.at[0, h, slot])
            )
            moves.append(
                pltpu.make_async_copy(tgt_hbm.at[rows, :], tbuf.at[slot, h], sems.at[1, h, slot])
            )
        return moves

    def fetch(p):
        @pl.when(p < groups)
        def _():
            for copy in copies(p, p & 1):
                copy.start()

    def arrive(p):
        @pl.when(p < groups)
        def _():
            for copy in copies(p, p & 1):
                copy.wait()

    fetch(0)
    if first:
        acc_ref[...] = jnp.zeros_like(acc_ref)
    else:
        acc_ref[...] = part_ref[...]
    rout_t = rout_ref[...].astype(F32).T.astype(BF16)
    atom_id = iota((BE, TE), 1).astype(F32)
    row_id = iota((CHUNK, TE), 0)

    def gather(p):
        for h in range(PER):
            j = begin + PER * p + h
            off = jnp.where(j < end, 0.0, 4096.0)
            j = jnp.maximum(jnp.minimum(j, end - 1), 0)
            c = jnp.clip(span_ref[2 * nb, j] - low, 0, count - 1)
            gate = lax.dot_general(
                rout_t, rbuf[p & 1, h], (((1,), (1,)), ((), ())), preferred_element_type=F32
            )
            pick = jnp.concatenate(
                [
                    as_bf16(row_id == src_ref[pl.ds(j * (BE // TE) + q, 1), :])
                    for q in range(BE // TE)
                ],
                axis=1,
            )
            rows = dot(tables[c], pick)
            for k in range(K):
                message = rows[cols(k), :] * gate[cols(degree_of[k]), :]
                message_ref[cols(k), h * BE : (h + 1) * BE] = message.astype(BF16)
            tgt = tbuf[p & 1, h].astype(F32) + off
            for q in range(ATOM_DEV // TE):
                land_ref[h * BE : (h + 1) * BE, q * TE : (q + 1) * TE] = as_bf16(
                    tgt == atom_id + float(q * TE)
                )

    for load in loads:
        load.wait()
    arrive(0)
    fetch(1)
    gather(0)

    def step(p, carry):
        arrive(p + 1)
        fetch(p + 2)
        acc_ref[...] += dot(message_ref[...], land_ref[...])
        gather(p + 1)
        return carry

    lax.fori_loop(0, groups, step, 0)
    if not final:
        return
    gate_sum = jnp.dot(
        rsum_ref[...],
        rout_ref[...].astype(F32),
        preferred_element_type=F32,
        precision=lax.Precision.HIGHEST,
    )
    for k in range(K):
        own = dot(x_ref[:, cols(k)], mix_ref[degree_of[k], C:])
        full = acc_ref[cols(k), :].T + own * gate_sum[:, cols(degree_of[k])]
        out_ref[:, cols(k)] = (inv_scale * full).astype(BF16)


def shape(dims, kind):
    return jax.ShapeDtypeStruct(dims, kind)


def cost(flops, size):
    return pl.CostEstimate(flops=int(flops), bytes_accessed=int(size), transcendentals=0)


def body(
    embedding,
    ghost_index,
    tile_count,
    edge_source,
    edge_target,
    edge_features,
    radial_in,
    radial_out,
    mix_weight,
):
    n_dom, n_tile = lax.axis_size("dom"), lax.axis_size("tile")
    tiles = edge_source.shape[0] // TE
    nb = 2 * n_tile
    slots = (tiles * TE // BE + nb) * BE
    count = lax.dynamic_slice_in_dim(tile_count[0], lax.axis_index("tile"), 1)
    source = edge_source.reshape(tiles, TE)
    target = edge_target.reshape(tiles, TE)
    hbm = pl.BlockSpec(memory_space=pl.ANY)

    mixed = pl.pallas_call(
        mix_kernel,
        out_shape=shape((WIDTH + EXTRA, ATOM_DEV), BF16),
        in_specs=[vmem(), vmem(), vmem()],
        out_specs=vmem(),
        compiler_params=PARAMS,
        cost_estimate=cost(256 * 256 * 1152, 2e6),
        name="mix",
    )(embedding, mix_weight, ghost_index.reshape(1, ATOM_DEV))
    ring = [(t, (t + 2) % n_tile) for t in range(n_tile)]
    flip = [(t, t ^ 1) for t in range(n_tile)]
    up = [(i, i + 1) for i in range(n_dom - 1)]
    down = [(i + 1, i) for i in range(n_dom - 1)]
    n_ring = n_tile // 2
    half = n_tile // 2

    tile_pos = lax.axis_index("tile")
    order = jnp.arange(nb, dtype=I32)
    quarter = order // half
    index = order - half * ((quarter + 1) // 2)
    steps, other = index // 2, index % 2
    origin = 2 * ((tile_pos // 2 - steps) % n_ring) + ((tile_pos % 2) ^ other)
    label = 2 * origin + quarter % 2
    label = jnp.broadcast_to(label[:, None], (nb, TE))

    pos, span = pl.pallas_call(
        functools.partial(rank_kernel, slots=slots),
        out_shape=(shape((tiles, TE), I32), shape((3 * nb, TE), I32)),
        in_specs=[smem(), vmem(), vmem()],
        out_specs=(vmem(), vmem()),
        scratch_shapes=[
            pltpu.VMEM((tiles * nb, TE), BF16),
            pltpu.VMEM((tiles * nb, 2 * TE), F32),
        ],
        compiler_params=PARAMS,
        cost_estimate=cost(4e9, 1e6),
        name="rank",
    )(count, source, label)
    radial, radial_sum = pl.pallas_call(
        radial_kernel,
        out_shape=(shape((tiles * TE, C), BF16), shape((ATOM_DEV, C), F32)),
        in_specs=[smem(), vmem(), vmem(), vmem()],
        out_specs=(vmem(), vmem()),
        compiler_params=PARAMS,
        cost_estimate=cost(10e9, 6e6),
        name="radial",
    )(count, target, edge_features, radial_in)

    def place(radial):
        return pl.pallas_call(
            place_kernel,
            out_shape=(
                shape((slots, C), BF16),
                shape((slots, C), BF16),
                shape((slots // TE, TE), I32),
            ),
            in_specs=[smem(), smem(), smem(), vmem(), vmem(), vmem()],
            out_specs=(vmem(), vmem(), vmem()),
            scratch_shapes=[
                pltpu.VMEM((2 * slots + 8, C), F32),
                pltpu.VMEM((2 * TE, C), F32),
                pltpu.VMEM((2 * TE, C), F32),
            ],
            compiler_params=PARAMS,
            cost_estimate=cost(20e9, 12e6),
            name="place",
        )(count, pos, span, source, target, radial)

    def pick(blocks):
        down_rows, up_rows = pl.pallas_call(
            pick_kernel,
            out_shape=(shape((len(blocks), WIDTH, GHOST), BF16),) * 2,
            in_specs=[vmem()] * len(blocks),
            out_specs=(vmem(), vmem()),
            compiler_params=PARAMS,
            cost_estimate=cost(3e9, 5e6),
            name="pick",
        )(*blocks)
        return [lax.ppermute(up_rows, "dom", up), lax.ppermute(down_rows, "dom", down)]

    def main(low, ghosts, owns, part, final_args, name):
        final = len(final_args) > 0
        dims, kind = ((ATOM_DEV, WIDTH), BF16) if final else ((WIDTH, ATOM_DEV), F32)
        n_ghost = half if ghosts else 0
        count_all = n_ghost + len(owns)
        extra = [*part, *final_args]
        return pl.pallas_call(
            functools.partial(
                main_kernel,
                low=low,
                n_ghost=n_ghost,
                n_own=len(owns),
                first=not part,
                final=final,
            ),
            out_shape=shape(dims, kind),
            in_specs=[smem()]
            + [hbm] * (len(ghosts) + len(owns) + 2)
            + [vmem()] * (2 + len(extra)),
            out_specs=vmem(),
            scratch_shapes=[
                pltpu.VMEM((2, PER, BE, C), BF16),
                pltpu.VMEM((2, PER, BE, C), BF16),
                pltpu.VMEM((PER * BE, ATOM_DEV), BF16),
                pltpu.VMEM((WIDTH, PER * BE), BF16),
                pltpu.VMEM((count_all, WIDTH, ATOM_DEV), BF16),
                pltpu.SemaphoreType.DMA((2, PER, 2)),
                pltpu.SemaphoreType.DMA((2 * n_ghost + len(owns),)),
            ]
            + ([pltpu.VMEM((WIDTH, ATOM_DEV), F32)] if final else []),
            compiler_params=PARAMS,
            cost_estimate=cost(3e9 * count_all, 2e6 * count_all),
            name=name,
        )(span, *ghosts, *owns, radial_sorted, target_sorted, source_sorted, radial_out, *extra)

    ring_rows, flip_rows = [mixed], []
    held = mixed
    for k in range(n_ring):
        flip_rows.append(lax.ppermute(held, "tile", flip))
        if k < n_ring - 1:
            held = lax.ppermute(held, "tile", ring)
            if k == 0:
                held, radial = lax.optimization_barrier((held, radial))
                radial_sorted, target_sorted, source_sorted = place(radial)
            if k == 1:
                held, radial_sorted = lax.optimization_barrier((held, radial_sorted))
            ring_rows.append(held)
    owns = [rows for pair in zip(ring_rows, flip_rows) for rows in pair]
    ghosts_a = pick(owns[:half])
    part = main(0, [], owns[:half], [], [], "main_own")
    owns_b = owns[half:]
    ghosts_b = pick(owns_b)
    part = main(half, ghosts_a, owns_b, [part], [], "main_mid")
    return main(
        n_tile + half, ghosts_b, [], [part], [radial_sum, embedding, mix_weight], "main_end"
    )


def solution(mesh):
    both = ("dom", "tile")
    return jax.shard_map(
        body,
        mesh=mesh,
        in_specs=(
            P(both, None),
            P(both),
            P("dom", None),
            P(both),
            P(both),
            P(both, None),
            P(),
            P(),
            P(),
        ),
        out_specs=P(both, None),
        check_vma=False,
    )
```

profile of v0, /device:TPU:26, one launch (start us, length us, event | category | flops | bytes accessed | tf_op | source)
XLA Modules:
  0.0 126.7 jit_solution(4173745287162034194)
XLA Ops:
  0.0 2.4 %mix.1.refs_0_.refs_1_ = bf16[1168,256]{1,0:T(8,128)(2,1)} custom-call(bf16[256,1152]{1,0:T(8,128)(2,1)} %refs_9_.1, bf16[3,256,128]{2,1,0:T(8,128)(2,1)} %refs_10_.3, s32[1,256]{1,0:T(1,128)} %bitcast.4), custom_call_target="tpu_custom_call" | custom-call | flops 75497472 | bytes 2000000 | tf_op jit(solution)/shard_map/mix/pallas_call | solution.py:351
  2.4 0.2 collective-permute-start
  2.6 1.5 %collective-permute-start.7 = (bf16[1168,256]{1,0:T(8,128)(2,1)}, bf16[1168,256]{1,0:T(8,128)(2,1)S(1)}, u32[]{:S(2)}, u32[]{:S(2)}) collective-permute-start(bf16[1168,256]{1,0:T(8,128)(2,1)} %mix.1.refs_0_.refs_1_), channel_id=1, source_target_pairs={{0,1},{1,0},{2,3},{3,2},{4,5},{5,4},{6,7},{7,6},{8,9},{9,8},{10,11... | collective-permute-start | bytes 1794056 | tf_op jit(solution)/shard_map/ppermute | solution.py:469
  4.2 0.6 constant_dynamic-slice_fusion
  4.8 14.3 %radial.1 = (bf16[12288,128]{1,0:T(8,128)(2,1)}, f32[256,128]{1,0:T(8,128)}) custom-call(s32[1]{0:T(128)} %bitcast.count_ref, s32[96,128]{1,0:T(8,128)} %bitcast.7, bf16[12288,128]{1,0:T(8,128)(2,1)} %feat_ref.1, bf16[128,128]{1,0:T(8,128)(2,1)} %rin_ref.1), custom_call_target="tpu_custom_call" | custom-call | flops 10000000000 | bytes 6000000 | tf_op jit(solution)/shard_map/radial/pallas_call | solution.py:389
  19.2 0.7 broadcast_in_dim.2.label_ref
  19.8 3.4 %rank.1 = (s32[96,128]{1,0:T(8,128)}, s32[48,128]{1,0:T(8,128)}) custom-call(s32[1]{0:T(128)} %bitcast.count_ref, s32[96,128]{1,0:T(8,128)} %bitcast.5, s32[16,128]{1,0:T(8,128)} %broadcast_in_dim.2.label_ref), custom_call_target="tpu_custom_call" | custom-call | flops 4000000000 | bytes 1000000 | tf_op jit(solution)/shard_map/rank/pallas_call | solution.py:376
  23.2 0.0 collective-permute-done.refs_2_.refs_3_
  23.2 0.1 collective-permute-start.1
  23.3 0.1 collective-permute-start.8
  23.4 22.7 %place.1 = (bf16[16384,128]{1,0:T(8,128)(2,1)}, bf16[16384,128]{1,0:T(8,128)(2,1)}, s32[128,128]{1,0:T(8,128)}) custom-call(s32[1]{0:T(128)} %bitcast.count_ref, s32[96,128]{1,0:T(8,128)} %get-tuple-element.23.pos_ref, s32[48,128]{1,0:T(8,128)} %get-tuple-element.20.span_ref.refs_0_, s32[96,128]{1,0:T(8,128)} %bitcast.6, s32[96,128]{1,0:T(8,128)} %bitcast.8, ...), custom_call_target="tpu_custom_call" | custom-call | flops 20000000000 | bytes 12000000 | tf_op jit(solution)/shard_map/place/pallas_call | solution.py:400
  46.0 0.1 collective-permute-start.3
  46.1 0.1 collective-permute-start.2
  46.2 0.8 copy-done.6
  47.1 0.8 copy-done.10
  47.9 3.9 %pick.3 = (bf16[4,1152,128]{2,1,0:T(8,128)(2,1)}, bf16[4,1152,128]{2,1,0:T(8,128)(2,1)}) custom-call(bf16[1168,256]{1,0:T(8,128)(2,1)} %mix.1.refs_0_.refs_1_, bf16[1168,256]{1,0:T(8,128)(2,1)} %copy-done.6, bf16[1168,256]{1,0:T(8,128)(2,1)} %copy-done.5, bf16[1168,256]{1,0:T(8,128)(2,1)} %copy-done.10), custom_call_target="tpu_custom_call" | custom-call | flops 3000000000 | bytes 5000000 | tf_op jit(solution)/shard_map/pick/pallas_call | solution.py:420
  51.8 3.8 %collective-permute-start.10 = (bf16[4,1152,128]{2,1,0:T(8,128)(2,1)}, bf16[4,1152,128]{2,1,0:T(8,128)(2,1)S(1)}, u32[]{:S(2)}, u32[]{:S(2)}) collective-permute-start(bf16[4,1152,128]{2,1,0:T(8,128)(2,1)} %get-tuple-element.33), channel_id=1, source_target_pairs={{8,0},{16,8},{24,16},{9,1},{17,9},{25,17},{10,2},{18,10},{26,18},{... | collective-permute-start | bytes 3538952 | tf_op jit(solution)/shard_map/ppermute | solution.py:429
  55.6 1.9 %collective-permute-start.9 = (bf16[4,1152,128]{2,1,0:T(8,128)(2,1)}, bf16[4,1152,128]{2,1,0:T(8,128)(2,1)S(1)}, u32[]{:S(2)}, u32[]{:S(2)}) collective-permute-start(bf16[4,1152,128]{2,1,0:T(8,128)(2,1)} %get-tuple-element.32), channel_id=1, source_target_pairs={{0,8},{8,16},{16,24},{1,9},{9,17},{17,25},{2,10},{10,18},{18,26},{... | collective-permute-start | bytes 3538952 | tf_op jit(solution)/shard_map/ppermute | solution.py:429
  57.5 3.2 %collective-permute-done.3.refs_2_.refs_5_ = bf16[1168,256]{1,0:T(8,128)(2,1)S(1)} collective-permute-done((bf16[1168,256]{1,0:T(8,128)(2,1)S(1)}, bf16[1168,256]{1,0:T(8,128)(2,1)S(1)}, u32[]{:S(2)}, u32[]{:S(2)}) %collective-permute-start.3) | collective-permute-done | bytes 598048 | tf_op jit(solution)/shard_map/ppermute | solution.py:471
  60.6 13.5 %main_own.1.refs_11_ = f32[1152,256]{1,0:T(8,128)} custom-call(s32[48,128]{1,0:T(8,128)} %get-tuple-element.20.span_ref.refs_0_, bf16[1168,256]{1,0:T(8,128)(2,1)} %mix.1.refs_0_.refs_1_, bf16[1168,256]{1,0:T(8,128)(2,1)} %copy-done.6, bf16[1168,256]{1,0:T(8,128)(2,1)} %copy-done.5, bf16[1168,256]{1,0:T(8,128)(2,1)} %copy-done.10, ...), custom_call_target="tpu_custom_call" | custom-call | flops 12000000000 | bytes 8000000 | tf_op jit(solution)/shard_map/main_own/pallas_call | solution.py:437
  74.2 0.0 collective-permute-done.4.refs_3_.refs_6_
  74.3 0.8 copy-done.9
  75.0 0.8 copy-done.11
  75.9 3.9 %pick.2 = (bf16[4,1152,128]{2,1,0:T(8,128)(2,1)}, bf16[4,1152,128]{2,1,0:T(8,128)(2,1)}) custom-call(bf16[1168,256]{1,0:T(8,128)(2,1)} %copy-done.7, bf16[1168,256]{1,0:T(8,128)(2,1)} %copy-done.9, bf16[1168,256]{1,0:T(8,128)(2,1)} %copy-done.8, bf16[1168,256]{1,0:T(8,128)(2,1)} %copy-done.11), custom_call_target="tpu_custom_call" | custom-call | flops 3000000000 | bytes 5000000 | tf_op jit(solution)/shard_map/pick/pallas_call | solution.py:420
  79.8 1.9 %collective-permute-start.5 = (bf16[4,1152,128]{2,1,0:T(8,128)(2,1)}, bf16[4,1152,128]{2,1,0:T(8,128)(2,1)S(1)}, u32[]{:S(2)}, u32[]{:S(2)}) collective-permute-start(bf16[4,1152,128]{2,1,0:T(8,128)(2,1)} %get-tuple-element.27), channel_id=1, source_target_pairs={{0,8},{8,16},{16,24},{1,9},{9,17},{17,25},{2,10},{10,18},{18,26},{... | collective-permute-start | bytes 3538952 | tf_op jit(solution)/shard_map/ppermute | solution.py:429
  81.7 3.6 %collective-permute-start.6 = (bf16[4,1152,128]{2,1,0:T(8,128)(2,1)}, bf16[4,1152,128]{2,1,0:T(8,128)(2,1)S(1)}, u32[]{:S(2)}, u32[]{:S(2)}) collective-permute-start(bf16[4,1152,128]{2,1,0:T(8,128)(2,1)} %get-tuple-element.28), channel_id=1, source_target_pairs={{8,0},{16,8},{24,16},{9,1},{17,9},{25,17},{10,2},{18,10},{26,18},{... | collective-permute-start | bytes 3538952 | tf_op jit(solution)/shard_map/ppermute | solution.py:429
  85.4 1.0 copy-done.1
  86.4 1.0 copy-done.2
  87.4 23.3 %main_mid.1.refs_7_ = f32[1152,256]{1,0:T(8,128)} custom-call(s32[48,128]{1,0:T(8,128)} %get-tuple-element.20.span_ref.refs_0_, bf16[4,1152,128]{2,1,0:T(8,128)(2,1)} %copy-done.2, bf16[4,1152,128]{2,1,0:T(8,128)(2,1)} %copy-done.1, bf16[1168,256]{1,0:T(8,128)(2,1)} %copy-done.7, bf16[1168,256]{1,0:T(8,128)(2,1)} %copy-done.9, bf16[1168,256]{1,0:T(8,128)(2,1)} %copy-done.8, ...), custom_call_target="tpu_custom_call" | custom-call | flops 24000000000 | bytes 16000000 | tf_op jit(solution)/shard_map/main_mid/pallas_call | solution.py:437
  110.7 1.0 copy-done.3
  111.7 0.4 copy-done.4
  112.0 14.5 %main_end.1 = bf16[256,1152]{1,0:T(8,128)(2,1)} custom-call(s32[48,128]{1,0:T(8,128)} %get-tuple-element.20.span_ref.refs_0_, bf16[4,1152,128]{2,1,0:T(8,128)(2,1)} %copy-done.3, bf16[4,1152,128]{2,1,0:T(8,128)(2,1)} %copy-done.4, bf16[16384,128]{1,0:T(8,128)(2,1)} %get-tuple-element.29.refs_5_.refs_7_.refs_3_, ...), custom_call_target="tpu_custom_call" | custom-call | flops 12000000000 | bytes 8000000 | tf_op jit(solution)/shard_map/main_end/pallas_call | solution.py:437
  (26 shorter events, 0.1 us)
Async XLA Ops:
  0.0 4.2 %copy-start = (s32[1,8]{1,0:T(1,128)S(1)}, s32[1,8]{1,0:T(1,128)}, u32[]{:S(2)}) copy-start(s32[1,8]{1,0:T(1,128)} %param.11) | copy-start | bytes 100
  2.4 20.8 %collective-permute-start = (bf16[1168,256]{1,0:T(8,128)(2,1)}, bf16[1168,256]{1,0:T(8,128)(2,1)S(1)}, u32[]{:S(2)}, u32[]{:S(2)}) collective-permute-start(bf16[1168,256]{1,0:T(8,128)(2,1)} %mix.1.refs_0_.refs_1_), channel_id=1, source_target_pairs={{0,2},{1,3},{2,4},{3,5},{4,6},{5,7},{6,0},{7,1},{8,10},{9,11},{10,... | collective-permute-start | bytes 1794056 | tf_op jit(solution)/shard_map/ppermute | solution.py:471
  2.6 43.5 %collective-permute-start.7 = (bf16[1168,256]{1,0:T(8,128)(2,1)}, bf16[1168,256]{1,0:T(8,128)(2,1)S(1)}, u32[]{:S(2)}, u32[]{:S(2)}) collective-permute-start(bf16[1168,256]{1,0:T(8,128)(2,1)} %mix.1.refs_0_.refs_1_), channel_id=1, source_target_pairs={{0,1},{1,0},{2,3},{3,2},{4,5},{5,4},{6,7},{7,6},{8,9},{9,8},{10,11... | collective-permute-start | bytes 1794056 | tf_op jit(solution)/shard_map/ppermute | solution.py:469
  23.2 22.8 %copy-start.5 = (bf16[1168,256]{1,0:T(8,128)(2,1)}, bf16[1168,256]{1,0:T(8,128)(2,1)S(1)}, u32[]{:S(2)}) copy-start(bf16[1168,256]{1,0:T(8,128)(2,1)S(1)} %collective-permute-done.refs_2_.refs_3_) | copy-start | bytes 1794052
  23.2 22.8 %collective-permute-start.1 = (bf16[1168,256]{1,0:T(8,128)(2,1)S(1)}, bf16[1168,256]{1,0:T(8,128)(2,1)S(1)}, u32[]{:S(2)}, u32[]{:S(2)}) collective-permute-start(bf16[1168,256]{1,0:T(8,128)(2,1)S(1)} %collective-permute-done.refs_2_.refs_3_), channel_id=1, source_target_pairs={{0,2},{1,3},{2,4},{3,5},{4,6},{5,7},{6,0},{7,1},{8,10},{9,11},{10,... | collective-permute-start | bytes 1794056 | tf_op jit(solution)/shard_map/ppermute | solution.py:471
  23.3 22.9 %collective-permute-start.8 = (bf16[1168,256]{1,0:T(8,128)(2,1)S(1)}, bf16[1168,256]{1,0:T(8,128)(2,1)S(1)}, u32[]{:S(2)}, u32[]{:S(2)}) collective-permute-start(bf16[1168,256]{1,0:T(8,128)(2,1)S(1)} %collective-permute-done.refs_2_.refs_3_), channel_id=1, source_target_pairs={{0,1},{1,0},{2,3},{3,2},{4,5},{5,4},{6,7},{7,6},{8,9},{9,8},{10,11... | collective-permute-start | bytes 1794056 | tf_op jit(solution)/shard_map/ppermute | solution.py:469
  46.0 5.8 %copy-start.7 = (bf16[1168,256]{1,0:T(8,128)(2,1)}, bf16[1168,256]{1,0:T(8,128)(2,1)S(1)}, u32[]{:S(2)}) copy-start(bf16[1168,256]{1,0:T(8,128)(2,1)S(1)} %collective-permute-done.1.refs_0_.refs_3_) | copy-start | bytes 1794052
  46.0 14.6 %collective-permute-start.3 = (bf16[1168,256]{1,0:T(8,128)(2,1)S(1)}, bf16[1168,256]{1,0:T(8,128)(2,1)S(1)}, u32[]{:S(2)}, u32[]{:S(2)}) collective-permute-start(bf16[1168,256]{1,0:T(8,128)(2,1)S(1)} %collective-permute-done.1.refs_0_.refs_3_), channel_id=1, source_target_pairs={{0,2},{1,3},{2,4},{3,5},{4,6},{5,7},{6,0},{7,1},{8,10},{9,11},{10,... | collective-permute-start | bytes 1794056 | tf_op jit(solution)/shard_map/ppermute | solution.py:471
  46.1 28.1 %collective-permute-start.2 = (bf16[1168,256]{1,0:T(8,128)(2,1)S(1)}, bf16[1168,256]{1,0:T(8,128)(2,1)S(1)}, u32[]{:S(2)}, u32[]{:S(2)}) collective-permute-start(bf16[1168,256]{1,0:T(8,128)(2,1)S(1)} %collective-permute-done.1.refs_0_.refs_3_), channel_id=1, source_target_pairs={{0,1},{1,0},{2,3},{3,2},{4,5},{5,4},{6,7},{7,6},{8,9},{9,8},{10,11... | collective-permute-start | bytes 1794056 | tf_op jit(solution)/shard_map/ppermute | solution.py:469
  46.2 0.9 copy-start.6
  47.1 0.8 copy-start.10
  51.8 33.5 %collective-permute-start.10 = (bf16[4,1152,128]{2,1,0:T(8,128)(2,1)}, bf16[4,1152,128]{2,1,0:T(8,128)(2,1)S(1)}, u32[]{:S(2)}, u32[]{:S(2)}) collective-permute-start(bf16[4,1152,128]{2,1,0:T(8,128)(2,1)} %get-tuple-element.33), channel_id=1, source_target_pairs={{8,0},{16,8},{24,16},{9,1},{17,9},{25,17},{10,2},{18,10},{26,18},{... | collective-permute-start | bytes 3538952 | tf_op jit(solution)/shard_map/ppermute | solution.py:429
  55.6 29.8 %collective-permute-start.9 = (bf16[4,1152,128]{2,1,0:T(8,128)(2,1)}, bf16[4,1152,128]{2,1,0:T(8,128)(2,1)S(1)}, u32[]{:S(2)}, u32[]{:S(2)}) collective-permute-start(bf16[4,1152,128]{2,1,0:T(8,128)(2,1)} %get-tuple-element.32), channel_id=1, source_target_pairs={{0,8},{8,16},{16,24},{1,9},{9,17},{17,25},{2,10},{10,18},{18,26},{... | collective-permute-start | bytes 3538952 | tf_op jit(solution)/shard_map/ppermute | solution.py:429
  60.6 13.6 %copy-start.8 = (bf16[1168,256]{1,0:T(8,128)(2,1)}, bf16[1168,256]{1,0:T(8,128)(2,1)S(1)}, u32[]{:S(2)}) copy-start(bf16[1168,256]{1,0:T(8,128)(2,1)S(1)} %collective-permute-done.3.refs_2_.refs_5_) | copy-start | bytes 1794052
  60.6 13.6 %collective-permute-start.4 = (bf16[1168,256]{1,0:T(8,128)(2,1)S(1)}, bf16[1168,256]{1,0:T(8,128)(2,1)S(1)}, u32[]{:S(2)}, u32[]{:S(2)}) collective-permute-start(bf16[1168,256]{1,0:T(8,128)(2,1)S(1)} %collective-permute-done.3.refs_2_.refs_5_), channel_id=1, source_target_pairs={{0,1},{1,0},{2,3},{3,2},{4,5},{5,4},{6,7},{7,6},{8,9},{9,8},{10,11... | collective-permute-start | bytes 1794056 | tf_op jit(solution)/shard_map/ppermute | solution.py:469
  74.2 0.8 copy-start.9
  75.0 0.9 copy-start.11
  79.8 30.9 %collective-permute-start.5 = (bf16[4,1152,128]{2,1,0:T(8,128)(2,1)}, bf16[4,1152,128]{2,1,0:T(8,128)(2,1)S(1)}, u32[]{:S(2)}, u32[]{:S(2)}) collective-permute-start(bf16[4,1152,128]{2,1,0:T(8,128)(2,1)} %get-tuple-element.27), channel_id=1, source_target_pairs={{0,8},{8,16},{16,24},{1,9},{9,17},{17,25},{2,10},{10,18},{18,26},{... | collective-permute-start | bytes 3538952 | tf_op jit(solution)/shard_map/ppermute | solution.py:429
  81.7 29.0 %collective-permute-start.6 = (bf16[4,1152,128]{2,1,0:T(8,128)(2,1)}, bf16[4,1152,128]{2,1,0:T(8,128)(2,1)S(1)}, u32[]{:S(2)}, u32[]{:S(2)}) collective-permute-start(bf16[4,1152,128]{2,1,0:T(8,128)(2,1)} %get-tuple-element.28), channel_id=1, source_target_pairs={{8,0},{16,8},{24,16},{9,1},{17,9},{25,17},{10,2},{18,10},{26,18},{... | collective-permute-start | bytes 3538952 | tf_op jit(solution)/shard_map/ppermute | solution.py:429
  85.3 1.0 copy-start.1
  86.4 1.0 copy-start.2
  110.6 1.0 copy-start.3
  110.7 1.4 %copy-start.4 = (bf16[4,1152,128]{2,1,0:T(8,128)(2,1)}, bf16[4,1152,128]{2,1,0:T(8,128)(2,1)S(1)}, u32[]{:S(2)}) copy-start(bf16[4,1152,128]{2,1,0:T(8,128)(2,1)S(1)} %collective-permute-done.6.refs_2_) | copy-start | bytes 3538948
where the time goes:
time: 127 us
  Pallas kernels  102 us (80%)
  starting transfers between devices  13.2 us (10%)
  local copies, waits for them, and re-layouts  7.99 us (6%)
  waiting for transfers between devices  3.21 us (3%)
    pallas_call x3, Pallas kernels, main(): pl.pallas_call(functools.partial(main_kernel, low=low, n_ghost=n_ghost, n...  51.3 us
    pallas_call x1, Pallas kernels, place(): pl.pallas_call(place_kernel, out_shape=(shape((slots, C), BF16), shape((s...  22.7 us
    pallas_call x1, Pallas kernels, body(): pl.pallas_call(radial_kernel, out_shape=(shape((tiles * TE, C), BF16), sh...  14.3 us
    pallas_call x2, Pallas kernels, pick(): pl.pallas_call(pick_kernel, out_shape=(shape((len(blocks), WIDTH, GHOST),...  7.78 us
    ppermute x2, starting transfers between devices, pick(): lax.ppermute(down_rows, 'dom', down)  7.4 us
    unnamed x24, local copies, waits for them, and re-layouts  6.69 us
    ppermute x2, starting transfers between devices, pick(): lax.ppermute(up_rows, 'dom', up)  3.83 us
    pallas_call x1, Pallas kernels, body(): pl.pallas_call(functools.partial(rank_kernel, slots=slots), out_shape=(sh...  3.36 us
  transfers between devices with their start and end apart: 11, of which 1 were waited for; matrix products, arithmetic and copies ran while one was open for 1% of the time, Pallas kernels for 67%

commit v1 on v0

--- a/solution.py
+++ b/solution.py
@@ -17,6 +17,7 @@
 WIDTH = K * C
 EXTRA = 16
 PER = 4
+FINISH = 2
 degree_of = (0, 1, 1, 1, 2, 2, 2, 2, 2)
 inv_scale = 0.125
 
@@ -24,7 +25,7 @@
 BF16 = jnp.bfloat16
 I32 = jnp.int32
 
-PARAMS = pltpu.CompilerParams(vmem_limit_bytes=58 * 1024 * 1024)
+PARAMS = pltpu.CompilerParams(vmem_limit_bytes=64 * 1024 * 1024)
 
 
 def vmem():
@@ -59,21 +60,55 @@
     mixed_ref[WIDTH:, :] = picks.astype(BF16)
 
 
-def pick_kernel(*refs):
-    *blocks, down_ref, up_ref = refs
-    for i, rows_ref in enumerate(blocks):
-        picks = rows_ref[WIDTH:, :].astype(F32)[:1, :].astype(I32)
-        chosen = as_bf16(iota((ATOM_DEV, 2 * GHOST), 0) == picks)
-        rows = dot(rows_ref[:WIDTH, :], chosen).astype(BF16)
-        down_ref[i] = rows[:, :GHOST]
-        up_ref[i] = rows[:, GHOST:]
-
-
-def rank_kernel(count_ref, src_ref, label_ref, pos_ref, span_ref, oh_ref, cum_ref, *, slots):
+def pick_kernel(*refs, n):
+    blocks, refs = refs[:n], refs[n:]
+    near_hbm, far_hbm, inside, near, far, sems = refs
+    even = (lax.axis_index("dom") & 1) == 0
+    loads = [
+        pltpu.make_async_copy(block, inside.at[i], sems.at[0, i]) for i, block in enumerate(blocks)
+    ]
+    saves = []
+    for load in loads:
+        load.start()
+    for i in range(n):
+        loads[i].wait()
+        picks = inside[i, WIDTH:, :].astype(F32)[:1, :].astype(I32)
+        down, up = picks[:, :GHOST], picks[:, GHOST:]
+        row_id = iota((ATOM_DEV, GHOST), 0)
+        chosen = jnp.concatenate(
+            [
+                as_bf16(row_id == jnp.where(even, up, down)),
+                as_bf16(row_id == jnp.where(even, down, up)),
+            ],
+            axis=1,
+        )
+        rows = dot(inside[i, :WIDTH, :], chosen).astype(BF16)
+        near[i] = rows[:, :GHOST]
+        far[i] = rows[:, GHOST:]
+        for side, (src, dst) in enumerate(((near, near_hbm), (far, far_hbm))):
+            save = pltpu.make_async_copy(src.at[i], dst.at[i], sems.at[1 + side, i])
+            save.start()
+            saves.append(save)
+    for save in saves:
+        save.wait()
+
+
+def live_tiles(count_ref):
+    return count_ref[0, lax.axis_index("tile")]
+
+
+def rank_kernel(count_ref, src_ref, pos_ref, span_ref, oh_ref, cum_ref, *, slots):
     tiles = src_ref.shape[0]
     nb = span_ref.shape[0] // 3
-    count = count_ref[0]
-    label = label_ref[...]
+    count = live_tiles(count_ref)
+    half, half_bits = nb // 4, (nb // 4).bit_length() - 1
+    order = iota((nb, TE), 0)
+    quarter = order >> half_bits
+    index = order - half * ((quarter + 1) >> 1)
+    tile_pos = lax.axis_index("tile")
+    ring_pos = (tile_pos >> 1) - (index >> 1)
+    ring_pos = jnp.where(ring_pos < 0, ring_pos + nb // 4, ring_pos)
+    label = 2 * (2 * ring_pos + ((tile_pos & 1) ^ (index & 1))) + (quarter & 1)
 
     def mark(t, carry):
         bucket = src_ref[pl.ds(t, 1), :] >> CHUNK_BITS
@@ -114,33 +149,59 @@
 
 def radial_kernel(count_ref, tgt_ref, feat_ref, rin_ref, rad_ref, rsum_ref):
     tiles = tgt_ref.shape[0]
-    count = count_ref[0]
+    count = live_tiles(count_ref)
     rsum_ref[...] = jnp.zeros_like(rsum_ref)
-    group = 4
+    group = 8
     atom_id = iota((ATOM_DEV, TE), 0)
 
-    def step(i, carry):
-        rows = pl.ds(pl.multiple_of(i * (group * TE), group * TE), group * TE)
-        hidden = dot(feat_ref[rows, :], rin_ref[...])
-        radial = (hidden / (1.0 + jnp.exp(-hidden))).astype(BF16)
-        rad_ref[rows, :] = radial
+    def rows_of(i):
+        return pl.ds(pl.multiple_of(i * (group * TE), group * TE), group * TE)
+
+    def hidden_layer(i):
+        hidden = 0.5 * dot(feat_ref[rows_of(i), :], rin_ref[...])
+        rad_ref[rows_of(i), :] = (hidden + hidden * jnp.tanh(hidden)).astype(BF16)
+
+    def add_up(i):
         land = []
         for q in range(group):
             t = i * group + q
             tgt = jnp.where(t < count, tgt_ref[pl.ds(t, 1), :], -1)
             land.append(as_bf16(atom_id == tgt))
-        rsum_ref[...] += dot(jnp.concatenate(land, axis=1), radial)
+        rsum_ref[...] += dot(jnp.concatenate(land, axis=1), rad_ref[rows_of(i), :])
+
+    hidden_layer(0)
+    groups = (count + group - 1) // group
+
+    def step(i, carry):
+        add_up(i)
+        hidden_layer(i + 1)
         return carry
 
-    lax.fori_loop(0, (count + group - 1) // group, step, 0)
+    lax.fori_loop(0, groups - 1, step, 0)
+    add_up(groups - 1)
 
 
 def place_kernel(
-    count_ref, pos_ref, span_ref, src_ref, tgt_ref, rin_ref, rad_ref, tgtb_ref, srcs_ref, pairs, even, odd
+    count_ref,
+    pos_ref,
+    span_ref,
+    src_ref,
+    tgt_ref,
+    rin_ref,
+    rad_hbm,
+    tgt_hbm,
+    srcs_ref,
+    pairs,
+    even,
+    odd,
+    rad_out,
+    tgt_out,
+    sems,
 ):
     tiles = src_ref.shape[0]
     nb = span_ref.shape[0] // 3
-    count = count_ref[0]
+    count = live_tiles(count_ref)
+    flip = jnp.where((lax.axis_index("dom") & 1) == 0, GHOST, 0)
     blank = jnp.where((iota((2 * BE, C), 0) & 1) == 1, -1.0, 0.0)
 
     def clear(b, carry):
@@ -163,7 +224,8 @@
         t = jnp.minimum(t, tiles - 1)
         rows = pl.ds(pl.multiple_of(t * TE, TE), TE)
         out[pl.ds(0, TE, stride=2), :] = rin_ref[rows, :].astype(F32)
-        src = src_ref[pl.ds(t, 1), :] & (CHUNK - 1)
+        src = src_ref[pl.ds(t, 1), :]
+        src = (src & (CHUNK - 1)) ^ jnp.where((src & CHUNK) != 0, flip, 0)
         tgt = tgt_ref[pl.ds(t, 1), :]
         diag_s = jnp.where(eye, src.astype(F32), 0.0).astype(BF16)
         diag_t = jnp.where(eye, tgt.astype(F32), 0.0).astype(BF16)
@@ -184,22 +246,45 @@
         return carry
 
     lax.fori_loop(0, (count + 1) // 2, step, 0)
+    many = FINISH * BE
+
+    def saves(j, slot):
+        rows = pl.ds(pl.multiple_of(j * many, many), many)
+        return (
+            pltpu.make_async_copy(rad_out.at[slot], rad_hbm.at[rows, :], sems.at[0, slot]),
+            pltpu.make_async_copy(tgt_out.at[slot], tgt_hbm.at[rows, :], sems.at[1, slot]),
+        )
 
     def finish(j, carry):
-        rows = pl.ds(pl.multiple_of(j * BE, BE), BE)
-        base = pl.multiple_of(j * (2 * BE), 2 * BE)
-        rad_ref[rows, :] = pairs[pl.ds(base, BE, stride=2), :].astype(BF16)
-        code = pairs[pl.ds(base + 1, BE, stride=2), :].astype(I32)
-        tgtb_ref[rows, :] = (code >> CHUNK_BITS).astype(F32).astype(BF16)
+        slot = j & 1
+
+        @pl.when(j >= 2)
+        def _():
+            for save in saves(j - 2, slot):
+                save.wait()
+
+        base = pl.multiple_of(j * (2 * many), 2 * many)
+        rad_out[slot] = pairs[pl.ds(base, many, stride=2), :].astype(BF16)
+        code = pairs[pl.ds(base + 1, many, stride=2), :].astype(I32)
+        tgt_out[slot] = (code >> CHUNK_BITS).astype(F32).astype(BF16)
         src = (code & (CHUNK - 1)).astype(F32)
-        for h in range(BE // TE):
+        for h in range(many // TE):
             part = jnp.where(eye, src[h * TE : (h + 1) * TE, :], 0.0)
-            row = pl.ds(j * (BE // TE) + h, 1)
+            row = pl.ds(j * (many // TE) + h, 1)
             srcs_ref[row, :] = jnp.sum(part, axis=0, keepdims=True).astype(I32)
+        for save in saves(j, slot):
+            save.start()
         return carry
 
     used = span_ref[nb - 1, 0] + span_ref[2 * nb - 1, 0]
-    lax.fori_loop(0, used, finish, 0)
+    steps = (used + FINISH - 1) // FINISH
+    lax.fori_loop(0, steps, finish, 0)
+    for back in (2, 1):
+
+        @pl.when(steps >= back)
+        def _():
+            for save in saves(steps - back, (steps - back) & 1):
+                save.wait()
 
 
 def main_kernel(*refs, low, n_ghost, n_own, first, final):
@@ -292,6 +377,9 @@
                     tgt == atom_id + float(q * TE)
                 )
 
+    def add_up():
+        acc_ref[...] += dot(message_ref[...], land_ref[...])
+
     for load in loads:
         load.wait()
     arrive(0)
@@ -301,11 +389,16 @@
     def step(p, carry):
         arrive(p + 1)
         fetch(p + 2)
-        acc_ref[...] += dot(message_ref[...], land_ref[...])
+        add_up()
         gather(p + 1)
         return carry
 
-    lax.fori_loop(0, groups, step, 0)
+    lax.fori_loop(0, groups - 1, step, 0)
+
+    @pl.when(groups > 0)
+    def _():
+        add_up()
+
     if not final:
         return
     gate_sum = jnp.dot(
@@ -343,7 +436,7 @@
     tiles = edge_source.shape[0] // TE
     nb = 2 * n_tile
     slots = (tiles * TE // BE + nb) * BE
-    count = lax.dynamic_slice_in_dim(tile_count[0], lax.axis_index("tile"), 1)
+    count = tile_count
     source = edge_source.reshape(tiles, TE)
     target = edge_target.reshape(tiles, TE)
     hbm = pl.BlockSpec(memory_space=pl.ANY)
@@ -359,24 +452,16 @@
     )(embedding, mix_weight, ghost_index.reshape(1, ATOM_DEV))
     ring = [(t, (t + 2) % n_tile) for t in range(n_tile)]
     flip = [(t, t ^ 1) for t in range(n_tile)]
-    up = [(i, i + 1) for i in range(n_dom - 1)]
-    down = [(i + 1, i) for i in range(n_dom - 1)]
+    near = [(i, i ^ 1) for i in range(n_dom)]
+    far = [(i, i + 1) for i in range(1, n_dom - 1, 2)]
+    far += [(j, i) for i, j in far]
     n_ring = n_tile // 2
     half = n_tile // 2
-
-    tile_pos = lax.axis_index("tile")
-    order = jnp.arange(nb, dtype=I32)
-    quarter = order // half
-    index = order - half * ((quarter + 1) // 2)
-    steps, other = index // 2, index % 2
-    origin = 2 * ((tile_pos // 2 - steps) % n_ring) + ((tile_pos % 2) ^ other)
-    label = 2 * origin + quarter % 2
-    label = jnp.broadcast_to(label[:, None], (nb, TE))
 
     pos, span = pl.pallas_call(
         functools.partial(rank_kernel, slots=slots),
         out_shape=(shape((tiles, TE), I32), shape((3 * nb, TE), I32)),
-        in_specs=[smem(), vmem(), vmem()],
+        in_specs=[smem(), vmem()],
         out_specs=(vmem(), vmem()),
         scratch_shapes=[
             pltpu.VMEM((tiles * nb, TE), BF16),
@@ -385,7 +470,7 @@
         compiler_params=PARAMS,
         cost_estimate=cost(4e9, 1e6),
         name="rank",
-    )(count, source, label)
+    )(count, source)
     radial, radial_sum = pl.pallas_call(
         radial_kernel,
         out_shape=(shape((tiles * TE, C), BF16), shape((ATOM_DEV, C), F32)),
@@ -405,11 +490,14 @@
                 shape((slots // TE, TE), I32),
             ),
             in_specs=[smem(), smem(), smem(), vmem(), vmem(), vmem()],
-            out_specs=(vmem(), vmem(), vmem()),
+            out_specs=(hbm, hbm, vmem()),
             scratch_shapes=[
                 pltpu.VMEM((2 * slots + 8, C), F32),
                 pltpu.VMEM((2 * TE, C), F32),
                 pltpu.VMEM((2 * TE, C), F32),
+                pltpu.VMEM((2, FINISH * BE, C), BF16),
+                pltpu.VMEM((2, FINISH * BE, C), BF16),
+                pltpu.SemaphoreType.DMA((2, 2)),
             ],
             compiler_params=PARAMS,
             cost_estimate=cost(20e9, 12e6),
@@ -417,16 +505,23 @@
         )(count, pos, span, source, target, radial)
 
     def pick(blocks):
-        down_rows, up_rows = pl.pallas_call(
-            pick_kernel,
-            out_shape=(shape((len(blocks), WIDTH, GHOST), BF16),) * 2,
-            in_specs=[vmem()] * len(blocks),
-            out_specs=(vmem(), vmem()),
+        n = len(blocks)
+        near_rows, far_rows = pl.pallas_call(
+            functools.partial(pick_kernel, n=n),
+            out_shape=(shape((n, WIDTH, GHOST), BF16),) * 2,
+            in_specs=[hbm] * n,
+            out_specs=(hbm, hbm),
+            scratch_shapes=[
+                pltpu.VMEM((n, WIDTH + EXTRA, ATOM_DEV), BF16),
+                pltpu.VMEM((n, WIDTH, GHOST), BF16),
+                pltpu.VMEM((n, WIDTH, GHOST), BF16),
+                pltpu.SemaphoreType.DMA((3, n)),
+            ],
             compiler_params=PARAMS,
             cost_estimate=cost(3e9, 5e6),
             name="pick",
         )(*blocks)
-        return [lax.ppermute(up_rows, "dom", up), lax.ppermute(down_rows, "dom", down)]
+        return [lax.ppermute(near_rows, "dom", near), lax.ppermute(far_rows, "dom", far)]
 
     def main(low, ghosts, owns, part, final_args, name):
         final = len(final_args) > 0

time: 127 us -> 117 us (0.921)
  the two profiles are of different devices: /device:TPU:26 before, /device:TPU:14 now
where the time goes in v1:
time: 117 us; the launch traced here: 115 us
  Pallas kernels  95.7 us (82%)
  starting transfers between devices  10.5 us (9%)
  waiting for transfers between devices  8.01 us (7%)
    pallas_call x3, Pallas kernels, main(): pl.pallas_call(functools.partial(main_kernel, low=low, n_ghost=n_ghost, n...  47.6 us
    pallas_call x1, Pallas kernels, place(): pl.pallas_call(place_kernel, out_shape=(shape((slots, C), BF16), shape((s...  27.3 us
    pallas_call x1, Pallas kernels, body(): pl.pallas_call(radial_kernel, out_shape=(shape((tiles * TE, C), BF16), sh...  7.99 us
    pallas_call x2, Pallas kernels, pick(): pl.pallas_call(functools.partial(pick_kernel, n=n), out_shape=(shape((n,...  7.71 us
    ppermute x3, waiting for transfers between devices, body(): held = lax.ppermute(held, 'tile', ring)  7.04 us
    ppermute x2, starting transfers between devices, pick(): lax.ppermute(far_rows, 'dom', far)  3.84 us
    ppermute x4, starting transfers between devices, body(): flip_rows.append(lax.ppermute(held, 'tile', flip))  3.27 us
    ppermute x3, starting transfers between devices, body(): held = lax.ppermute(held, 'tile', ring)  3.21 us
  transfers between devices with their start and end apart: 11, of which 3 were waited for; matrix products, arithmetic and copies ran while one was open for 0% of the time, Pallas kernels for 70%

profile of v1, /device:TPU:14, one launch (start us, length us, event | category | flops | bytes accessed | tf_op | source)
XLA Modules:
  0.0 114.5 jit_solution(15915815542647601357)
XLA Ops:
  0.0 2.4 %mix.1.refs_0_.refs_1_ = bf16[1168,256]{1,0:T(8,128)(2,1)} custom-call(bf16[256,1152]{1,0:T(8,128)(2,1)} %refs_9_.1, bf16[3,256,128]{2,1,0:T(8,128)(2,1)} %refs_10_.3, s32[1,256]{1,0:T(1,128)} %bitcast.3), custom_call_target="tpu_custom_call" | custom-call | flops 75497472 | bytes 2000000 | tf_op jit(solution)/shard_map/mix/pallas_call | solution.py:444
  2.4 1.6 %collective-permute-start = (bf16[1168,256]{1,0:T(8,128)(2,1)}, bf16[1168,256]{1,0:T(8,128)(2,1)}, u32[]{:S(2)}, u32[]{:S(2)}) collective-permute-start(bf16[1168,256]{1,0:T(8,128)(2,1)} %mix.1.refs_0_.refs_1_), channel_id=1, source_target_pairs={{0,2},{1,3},{2,4},{3,5},{4,6},{5,7},{6,0},{7,1},{8,10},{9,11},{10,... | collective-permute-start | bytes 1794056 | tf_op jit(solution)/shard_map/ppermute | solution.py:566
  4.0 0.5 collective-permute-start.7
  4.5 8.0 %radial.1 = (bf16[12288,128]{1,0:T(8,128)(2,1)}, f32[256,128]{1,0:T(8,128)}) custom-call(s32[1,8]{1,0:T(1,128)} %count_ref.5, s32[96,128]{1,0:T(8,128)} %bitcast.6, bf16[12288,128]{1,0:T(8,128)(2,1)} %feat_ref.1, bf16[128,128]{1,0:T(8,128)(2,1)} %rin_ref.1), custom_call_target="tpu_custom_call" | custom-call | flops 10000000000 | bytes 6000000 | tf_op jit(solution)/shard_map/radial/pallas_call | solution.py:474
  12.5 2.8 %rank.1 = (s32[96,128]{1,0:T(8,128)}, s32[48,128]{1,0:T(8,128)}) custom-call(s32[1,8]{1,0:T(1,128)} %count_ref.5, s32[96,128]{1,0:T(8,128)} %bitcast.4), custom_call_target="tpu_custom_call" | custom-call | flops 4000000000 | bytes 1000000 | tf_op jit(solution)/shard_map/rank/pallas_call | solution.py:461
  15.2 2.7 %collective-permute-done.refs_2_.refs_3_ = bf16[1168,256]{1,0:T(8,128)(2,1)} collective-permute-done((bf16[1168,256]{1,0:T(8,128)(2,1)}, bf16[1168,256]{1,0:T(8,128)(2,1)}, u32[]{:S(2)}, u32[]{:S(2)}) %collective-permute-start) | collective-permute-done | bytes 598048 | tf_op jit(solution)/shard_map/ppermute | solution.py:566
  17.9 1.6 %collective-permute-start.1 = (bf16[1168,256]{1,0:T(8,128)(2,1)}, bf16[1168,256]{1,0:T(8,128)(2,1)}, u32[]{:S(2)}, u32[]{:S(2)}) collective-permute-start(bf16[1168,256]{1,0:T(8,128)(2,1)} %collective-permute-done.refs_2_.refs_3_), channel_id=1, source_target_pairs={{0,2},{1,3},{2,4},{3,5},{4,6},{5,7},{6,0},{7,1},{8,10},{9,11},{10,... | collective-permute-start | bytes 1794056 | tf_op jit(solution)/shard_map/ppermute | solution.py:566
  19.5 0.5 collective-permute-start.8
  20.0 27.3 %place.1 = (bf16[16384,128]{1,0:T(8,128)(2,1)}, bf16[16384,128]{1,0:T(8,128)(2,1)}, s32[128,128]{1,0:T(8,128)}) custom-call(s32[1,8]{1,0:T(1,128)} %count_ref.5, s32[96,128]{1,0:T(8,128)} %get-tuple-element.23.pos_ref, s32[48,128]{1,0:T(8,128)} %get-tuple-element.20.span_ref.refs_0_, s32[96,128]{1,0:T(8,128)} %bitcast.5, s32[96,128]{1,0:T(8,128)} %bitcast.7, ...), custom_call_target="tpu_custom_call" | custom-call | flops 20000000000 | bytes 12000000 | tf_op jit(solution)/shard_map/place/pallas_call | solution.py:485
  47.3 0.0 collective-permute-done.1.refs_0_.refs_3_
  47.3 0.1 collective-permute-start.3
  47.4 0.1 collective-permute-start.2
  47.5 0.0 collective-permute-done.7.refs_1_.refs_2_
  47.5 0.0 collective-permute-done.8.refs_3_.refs_4_
  47.5 3.8 %pick.3 = (bf16[4,1152,128]{2,1,0:T(8,128)(2,1)}, bf16[4,1152,128]{2,1,0:T(8,128)(2,1)}) custom-call(bf16[1168,256]{1,0:T(8,128)(2,1)} %mix.1.refs_0_.refs_1_, bf16[1168,256]{1,0:T(8,128)(2,1)} %collective-permute-done.7.refs_1_.refs_2_, bf16[1168,256]{1,0:T(8,128)(2,1)} %collective-permute-done.refs_2_.refs_3_, ...), custom_call_target="tpu_custom_call" | custom-call | flops 3000000000 | bytes 5000000 | tf_op jit(solution)/shard_map/pick/pallas_call | solution.py:509
  51.3 1.9 %collective-permute-start.10 = (bf16[4,1152,128]{2,1,0:T(8,128)(2,1)}, bf16[4,1152,128]{2,1,0:T(8,128)(2,1)}, u32[]{:S(2)}, u32[]{:S(2)}) collective-permute-start(bf16[4,1152,128]{2,1,0:T(8,128)(2,1)} %get-tuple-element.33), channel_id=1, source_target_pairs={{8,16},{16,8},{9,17},{17,9},{10,18},{18,10},{11,19},{19,11},{12,20... | collective-permute-start | bytes 3538952 | tf_op jit(solution)/shard_map/ppermute | solution.py:524
  53.3 0.1 collective-permute-start.9
  53.4 4.3 %collective-permute-done.3.refs_2_.refs_5_ = bf16[1168,256]{1,0:T(8,128)(2,1)} collective-permute-done((bf16[1168,256]{1,0:T(8,128)(2,1)}, bf16[1168,256]{1,0:T(8,128)(2,1)}, u32[]{:S(2)}, u32[]{:S(2)}) %collective-permute-start.3) | collective-permute-done | bytes 598048 | tf_op jit(solution)/shard_map/ppermute | solution.py:566
  57.7 2.2 %collective-permute-start.4 = (bf16[1168,256]{1,0:T(8,128)(2,1)}, bf16[1168,256]{1,0:T(8,128)(2,1)}, u32[]{:S(2)}, u32[]{:S(2)}) collective-permute-start(bf16[1168,256]{1,0:T(8,128)(2,1)} %collective-permute-done.3.refs_2_.refs_5_), channel_id=1, source_target_pairs={{0,1},{1,0},{2,3},{3,2},{4,5},{5,4},{6,7},{7,6},{8,9},{9,8},{10,11... | collective-permute-start | bytes 1794056 | tf_op jit(solution)/shard_map/ppermute | solution.py:564
  59.9 12.3 %main_own.1.refs_11_ = f32[1152,256]{1,0:T(8,128)} custom-call(s32[48,128]{1,0:T(8,128)} %get-tuple-element.20.span_ref.refs_0_, bf16[1168,256]{1,0:T(8,128)(2,1)} %mix.1.refs_0_.refs_1_, bf16[1168,256]{1,0:T(8,128)(2,1)} %collective-permute-done.7.refs_1_.refs_2_, bf16[1168,256]{1,0:T(8,128)(2,1)} %collective-permute-done.refs_2_.refs_3_, ...), custom_call_target="tpu_custom_call" | custom-call | flops 12000000000 | bytes 8000000 | tf_op jit(solution)/shard_map/main_own/pallas_call | solution.py:532
  72.2 0.0 collective-permute-done.2.refs_1_.refs_4_
  72.2 0.9 collective-permute-done.4.refs_3_.refs_6_
  73.2 3.9 %pick.2 = (bf16[4,1152,128]{2,1,0:T(8,128)(2,1)}, bf16[4,1152,128]{2,1,0:T(8,128)(2,1)}) custom-call(bf16[1168,256]{1,0:T(8,128)(2,1)} %collective-permute-done.1.refs_0_.refs_3_, bf16[1168,256]{1,0:T(8,128)(2,1)} %collective-permute-done.2.refs_1_.refs_4_, bf16[1168,256]{1,0:T(8,128)(2,1)} %collective-permute-done.3.refs_2_.refs_5_, ...), custom_call_target="tpu_custom_call" | custom-call | flops 3000000000 | bytes 5000000 | tf_op jit(solution)/shard_map/pick/pallas_call | solution.py:509
  77.0 0.1 collective-permute-start.5
  77.1 1.9 %collective-permute-start.6 = (bf16[4,1152,128]{2,1,0:T(8,128)(2,1)}, bf16[4,1152,128]{2,1,0:T(8,128)(2,1)}, u32[]{:S(2)}, u32[]{:S(2)}) collective-permute-start(bf16[4,1152,128]{2,1,0:T(8,128)(2,1)} %get-tuple-element.28), channel_id=1, source_target_pairs={{8,16},{16,8},{9,17},{17,9},{10,18},{18,10},{11,19},{19,11},{12,20... | collective-permute-start | bytes 3538952 | tf_op jit(solution)/shard_map/ppermute | solution.py:524
  79.0 0.0 collective-permute-done.10.refs_2_
  79.0 0.0 collective-permute-done.9.refs_1_
  79.1 21.9 %main_mid.1.refs_7_ = f32[1152,256]{1,0:T(8,128)} custom-call(s32[48,128]{1,0:T(8,128)} %get-tuple-element.20.span_ref.refs_0_, bf16[4,1152,128]{2,1,0:T(8,128)(2,1)} %collective-permute-done.9.refs_1_, bf16[4,1152,128]{2,1,0:T(8,128)(2,1)} %collective-permute-done.10.refs_2_, bf16[1168,256]{1,0:T(8,128)(2,1)} %collective-permute-done.1.refs_0_.refs_3_, ...), custom_call_target="tpu_custom_call" | custom-call | flops 24000000000 | bytes 16000000 | tf_op jit(solution)/shard_map/main_mid/pallas_call | solution.py:532
  101.0 0.0 collective-permute-done.5.refs_1_
  101.0 0.0 collective-permute-done.6.refs_2_
  101.0 13.3 %main_end.1 = bf16[256,1152]{1,0:T(8,128)(2,1)} custom-call(s32[48,128]{1,0:T(8,128)} %get-tuple-element.20.span_ref.refs_0_, bf16[4,1152,128]{2,1,0:T(8,128)(2,1)} %collective-permute-done.5.refs_1_, bf16[4,1152,128]{2,1,0:T(8,128)(2,1)} %collective-permute-done.6.refs_2_, bf16[16384,128]{1,0:T(8,128)(2,1)} %get-tuple-element.29.refs_5_.refs_7_.refs_3_, ...), custom_call_target="tpu_custom_call" | custom-call | flops 12000000000 | bytes 8000000 | tf_op jit(solution)/shard_map/main_end/pallas_call | solution.py:532
Async XLA Ops:
  2.4 15.6 %collective-permute-start = (bf16[1168,256]{1,0:T(8,128)(2,1)}, bf16[1168,256]{1,0:T(8,128)(2,1)}, u32[]{:S(2)}, u32[]{:S(2)}) collective-permute-start(bf16[1168,256]{1,0:T(8,128)(2,1)} %mix.1.refs_0_.refs_1_), channel_id=1, source_target_pairs={{0,2},{1,3},{2,4},{3,5},{4,6},{5,7},{6,0},{7,1},{8,10},{9,11},{10,... | collective-permute-start | bytes 1794056 | tf_op jit(solution)/shard_map/ppermute | solution.py:566
  4.0 43.5 %collective-permute-start.7 = (bf16[1168,256]{1,0:T(8,128)(2,1)}, bf16[1168,256]{1,0:T(8,128)(2,1)}, u32[]{:S(2)}, u32[]{:S(2)}) collective-permute-start(bf16[1168,256]{1,0:T(8,128)(2,1)} %mix.1.refs_0_.refs_1_), channel_id=1, source_target_pairs={{0,1},{1,0},{2,3},{3,2},{4,5},{5,4},{6,7},{7,6},{8,9},{9,8},{10,11... | collective-permute-start | bytes 1794056 | tf_op jit(solution)/shard_map/ppermute | solution.py:564
  17.9 29.4 %collective-permute-start.1 = (bf16[1168,256]{1,0:T(8,128)(2,1)}, bf16[1168,256]{1,0:T(8,128)(2,1)}, u32[]{:S(2)}, u32[]{:S(2)}) collective-permute-start(bf16[1168,256]{1,0:T(8,128)(2,1)} %collective-permute-done.refs_2_.refs_3_), channel_id=1, source_target_pairs={{0,2},{1,3},{2,4},{3,5},{4,6},{5,7},{6,0},{7,1},{8,10},{9,11},{10,... | collective-permute-start | bytes 1794056 | tf_op jit(solution)/shard_map/ppermute | solution.py:566
  19.5 28.0 %collective-permute-start.8 = (bf16[1168,256]{1,0:T(8,128)(2,1)}, bf16[1168,256]{1,0:T(8,128)(2,1)}, u32[]{:S(2)}, u32[]{:S(2)}) collective-permute-start(bf16[1168,256]{1,0:T(8,128)(2,1)} %collective-permute-done.refs_2_.refs_3_), channel_id=1, source_target_pairs={{0,1},{1,0},{2,3},{3,2},{4,5},{5,4},{6,7},{7,6},{8,9},{9,8},{10,11... | collective-permute-start | bytes 1794056 | tf_op jit(solution)/shard_map/ppermute | solution.py:564
  47.3 10.3 %collective-permute-start.3 = (bf16[1168,256]{1,0:T(8,128)(2,1)}, bf16[1168,256]{1,0:T(8,128)(2,1)}, u32[]{:S(2)}, u32[]{:S(2)}) collective-permute-start(bf16[1168,256]{1,0:T(8,128)(2,1)} %collective-permute-done.1.refs_0_.refs_3_), channel_id=1, source_target_pairs={{0,2},{1,3},{2,4},{3,5},{4,6},{5,7},{6,0},{7,1},{8,10},{9,11},{10,... | collective-permute-start | bytes 1794056 | tf_op jit(solution)/shard_map/ppermute | solution.py:566
  47.4 24.8 %collective-permute-start.2 = (bf16[1168,256]{1,0:T(8,128)(2,1)}, bf16[1168,256]{1,0:T(8,128)(2,1)}, u32[]{:S(2)}, u32[]{:S(2)}) collective-permute-start(bf16[1168,256]{1,0:T(8,128)(2,1)} %collective-permute-done.1.refs_0_.refs_3_), channel_id=1, source_target_pairs={{0,1},{1,0},{2,3},{3,2},{4,5},{5,4},{6,7},{7,6},{8,9},{9,8},{10,11... | collective-permute-start | bytes 1794056 | tf_op jit(solution)/shard_map/ppermute | solution.py:564
  51.3 27.7 %collective-permute-start.10 = (bf16[4,1152,128]{2,1,0:T(8,128)(2,1)}, bf16[4,1152,128]{2,1,0:T(8,128)(2,1)}, u32[]{:S(2)}, u32[]{:S(2)}) collective-permute-start(bf16[4,1152,128]{2,1,0:T(8,128)(2,1)} %get-tuple-element.33), channel_id=1, source_target_pairs={{8,16},{16,8},{9,17},{17,9},{10,18},{18,10},{11,19},{19,11},{12,20... | collective-permute-start | bytes 3538952 | tf_op jit(solution)/shard_map/ppermute | solution.py:524
  53.3 25.8 %collective-permute-start.9 = (bf16[4,1152,128]{2,1,0:T(8,128)(2,1)}, bf16[4,1152,128]{2,1,0:T(8,128)(2,1)}, u32[]{:S(2)}, u32[]{:S(2)}) collective-permute-start(bf16[4,1152,128]{2,1,0:T(8,128)(2,1)} %get-tuple-element.32), channel_id=1, source_target_pairs={{0,8},{8,0},{16,24},{24,16},{1,9},{9,1},{17,25},{25,17},{2,10},{10... | collective-permute-start | bytes 3538952 | tf_op jit(solution)/shard_map/ppermute | solution.py:524
  57.7 15.5 %collective-permute-start.4 = (bf16[1168,256]{1,0:T(8,128)(2,1)}, bf16[1168,256]{1,0:T(8,128)(2,1)}, u32[]{:S(2)}, u32[]{:S(2)}) collective-permute-start(bf16[1168,256]{1,0:T(8,128)(2,1)} %collective-permute-done.3.refs_2_.refs_5_), channel_id=1, source_target_pairs={{0,1},{1,0},{2,3},{3,2},{4,5},{5,4},{6,7},{7,6},{8,9},{9,8},{10,11... | collective-permute-start | bytes 1794056 | tf_op jit(solution)/shard_map/ppermute | solution.py:564
  77.0 24.0 %collective-permute-start.5 = (bf16[4,1152,128]{2,1,0:T(8,128)(2,1)}, bf16[4,1152,128]{2,1,0:T(8,128)(2,1)}, u32[]{:S(2)}, u32[]{:S(2)}) collective-permute-start(bf16[4,1152,128]{2,1,0:T(8,128)(2,1)} %get-tuple-element.27), channel_id=1, source_target_pairs={{0,8},{8,0},{16,24},{24,16},{1,9},{9,1},{17,25},{25,17},{2,10},{10... | collective-permute-start | bytes 3538952 | tf_op jit(solution)/shard_map/ppermute | solution.py:524
  77.1 23.9 %collective-permute-start.6 = (bf16[4,1152,128]{2,1,0:T(8,128)(2,1)}, bf16[4,1152,128]{2,1,0:T(8,128)(2,1)}, u32[]{:S(2)}, u32[]{:S(2)}) collective-permute-start(bf16[4,1152,128]{2,1,0:T(8,128)(2,1)} %get-tuple-element.28), channel_id=1, source_target_pairs={{8,16},{16,8},{9,17},{17,9},{10,18},{18,10},{11,19},{19,11},{12,20... | collective-permute-start | bytes 3538952 | tf_op jit(solution)/shard_map/ppermute | solution.py:524

commit v2 on v1

--- a/solution.py
+++ b/solution.py
@@ -17,7 +17,6 @@
 WIDTH = K * C
 EXTRA = 16
 PER = 4
-FINISH = 2
 degree_of = (0, 1, 1, 1, 2, 2, 2, 2, 2)
 inv_scale = 0.125
 
@@ -101,14 +100,16 @@
     tiles = src_ref.shape[0]
     nb = span_ref.shape[0] // 3
     count = live_tiles(count_ref)
-    half, half_bits = nb // 4, (nb // 4).bit_length() - 1
+    owns, half = nb // 2, nb // 4
     order = iota((nb, TE), 0)
-    quarter = order >> half_bits
-    index = order - half * ((quarter + 1) >> 1)
+    ghost = ((order >= owns - 1) & (order < owns - 1 + half)) | (order >= owns + half)
+    index = jnp.where(order >= owns - 1, order - (owns - 1), order)
+    index = jnp.where(order == owns - 1 + half, owns - 1, index)
+    index = jnp.where(order >= owns + half, order - owns, index)
     tile_pos = lax.axis_index("tile")
     ring_pos = (tile_pos >> 1) - (index >> 1)
-    ring_pos = jnp.where(ring_pos < 0, ring_pos + nb // 4, ring_pos)
-    label = 2 * (2 * ring_pos + ((tile_pos & 1) ^ (index & 1))) + (quarter & 1)
+    ring_pos = jnp.where(ring_pos < 0, ring_pos + half, ring_pos)
+    label = 2 * (2 * ring_pos + ((tile_pos & 1) ^ (index & 1))) + jnp.where(ghost, 1, 0)
 
     def mark(t, carry):
         bucket = src_ref[pl.ds(t, 1), :] >> CHUNK_BITS
@@ -246,45 +247,38 @@
         return carry
 
     lax.fori_loop(0, (count + 1) // 2, step, 0)
-    many = FINISH * BE
-
-    def saves(j, slot):
-        rows = pl.ds(pl.multiple_of(j * many, many), many)
+
+    def saves(j):
+        rows = pl.ds(pl.multiple_of(j * BE, BE), BE)
         return (
-            pltpu.make_async_copy(rad_out.at[slot], rad_hbm.at[rows, :], sems.at[0, slot]),
-            pltpu.make_async_copy(tgt_out.at[slot], tgt_hbm.at[rows, :], sems.at[1, slot]),
+            pltpu.make_async_copy(rad_out.at[rows, :], rad_hbm.at[rows, :], sems.at[0, j]),
+            pltpu.make_async_copy(tgt_out.at[rows, :], tgt_hbm.at[rows, :], sems.at[1, j]),
         )
 
     def finish(j, carry):
-        slot = j & 1
-
-        @pl.when(j >= 2)
-        def _():
-            for save in saves(j - 2, slot):
-                save.wait()
-
-        base = pl.multiple_of(j * (2 * many), 2 * many)
-        rad_out[slot] = pairs[pl.ds(base, many, stride=2), :].astype(BF16)
-        code = pairs[pl.ds(base + 1, many, stride=2), :].astype(I32)
-        tgt_out[slot] = (code >> CHUNK_BITS).astype(F32).astype(BF16)
-        src = (code & (CHUNK - 1)).astype(F32)
-        for h in range(many // TE):
-            part = jnp.where(eye, src[h * TE : (h + 1) * TE, :], 0.0)
-            row = pl.ds(j * (many // TE) + h, 1)
-            srcs_ref[row, :] = jnp.sum(part, axis=0, keepdims=True).astype(I32)
-        for save in saves(j, slot):
+        for h in range(BE // TE):
+            row = j * (BE // TE) + h
+            rows = pl.ds(pl.multiple_of(row * TE, TE), TE)
+            base = pl.multiple_of(row * (2 * TE), 2 * TE)
+            rad_out[rows, :] = pairs[pl.ds(base, TE, stride=2), :].astype(BF16)
+            code = pairs[pl.ds(base + 1, TE, stride=2), :]
+            tgt = jnp.floor(code * (1.0 / CHUNK))
+            tgt_out[rows, :] = tgt.astype(BF16)
+            src = jnp.where(eye, code - CHUNK * tgt, 0.0)
+            srcs_ref[pl.ds(row, 1), :] = jnp.sum(src, axis=0, keepdims=True).astype(I32)
+        for save in saves(j):
             save.start()
         return carry
 
     used = span_ref[nb - 1, 0] + span_ref[2 * nb - 1, 0]
-    steps = (used + FINISH - 1) // FINISH
-    lax.fori_loop(0, steps, finish, 0)
-    for back in (2, 1):
-
-        @pl.when(steps >= back)
-        def _():
-            for save in saves(steps - back, (steps - back) & 1):
-                save.wait()
+    lax.fori_loop(0, used, finish, 0)
+
+    def drain(j, carry):
+        for save in saves(j):
+            save.wait()
+        return carry
+
+    lax.fori_loop(0, used, drain, 0)
 
 
 def main_kernel(*refs, low, n_ghost, n_own, first, final):
@@ -495,9 +489,9 @@
                 pltpu.VMEM((2 * slots + 8, C), F32),
                 pltpu.VMEM((2 * TE, C), F32),
                 pltpu.VMEM((2 * TE, C), F32),
-                pltpu.VMEM((2, FINISH * BE, C), BF16),
-                pltpu.VMEM((2, FINISH * BE, C), BF16),
-                pltpu.SemaphoreType.DMA((2, 2)),
+                pltpu.VMEM((slots, C), BF16),
+                pltpu.VMEM((slots, C), BF16),
+                pltpu.SemaphoreType.DMA((2, slots // BE)),
             ],
             compiler_params=PARAMS,
             cost_estimate=cost(20e9, 12e6),
@@ -518,10 +512,10 @@
                 pltpu.SemaphoreType.DMA((3, n)),
             ],
             compiler_params=PARAMS,
-            cost_estimate=cost(3e9, 5e6),
+            cost_estimate=cost(2e8, 4e5),
             name="pick",
         )(*blocks)
-        return [lax.ppermute(near_rows, "dom", near), lax.ppermute(far_rows, "dom", far)]
+        return near_rows, far_rows
 
     def main(low, ghosts, owns, part, final_args, name):
         final = len(final_args) > 0
@@ -554,30 +548,44 @@
             ]
             + ([pltpu.VMEM((WIDTH, ATOM_DEV), F32)] if final else []),
             compiler_params=PARAMS,
-            cost_estimate=cost(3e9 * count_all, 2e6 * count_all),
+            cost_estimate=cost(1e8 * count_all, 1e5 * count_all),
             name=name,
         )(span, *ghosts, *owns, radial_sorted, target_sorted, source_sorted, radial_out, *extra)
 
+    together = lax.optimization_barrier
     ring_rows, flip_rows = [mixed], []
     held = mixed
+    part = None
     for k in range(n_ring):
+        if k == n_ring - 1:
+            early = [rows for pair in zip(ring_rows, flip_rows) for rows in pair]
+            early.append(ring_rows[half // 2])
+            part = main(0, [], early[: half + 1], [], [], "main_one")
+            held, part = together((held, part))
+            ring_rows[-1] = held
         flip_rows.append(lax.ppermute(held, "tile", flip))
         if k < n_ring - 1:
             held = lax.ppermute(held, "tile", ring)
             if k == 0:
-                held, radial = lax.optimization_barrier((held, radial))
+                held, radial = together((held, radial))
                 radial_sorted, target_sorted, source_sorted = place(radial)
             if k == 1:
-                held, radial_sorted = lax.optimization_barrier((held, radial_sorted))
+                held, radial_sorted = together((held, radial_sorted))
             ring_rows.append(held)
     owns = [rows for pair in zip(ring_rows, flip_rows) for rows in pair]
-    ghosts_a = pick(owns[:half])
-    part = main(0, [], owns[:half], [], [], "main_own")
-    owns_b = owns[half:]
-    ghosts_b = pick(owns_b)
-    part = main(half, ghosts_a, owns_b, [part], [], "main_mid")
+
+    def pick_after(blocks, part):
+        first, part = together((blocks[0], part))
+        near_rows, far_rows = pick([first, *blocks[1:]])
+        near_rows, part = together((near_rows, part))
+        return [lax.ppermute(near_rows, "dom", near), lax.ppermute(far_rows, "dom", far)], part
+
+    ghosts_a, part = pick_after(owns[:half], part)
+    part = main(half + 1, [], owns[half + 1 : -1], [part], [], "main_two")
+    ghosts_b, part = pick_after(owns[half:], part)
+    part = main(n_tile - 1, ghosts_a, owns[-1:], [part], [], "main_three")
     return main(
-        n_tile + half, ghosts_b, [], [part], [radial_sum, embedding, mix_weight], "main_end"
+        n_tile + half, ghosts_b, [], [part], [radial_sum, embedding, mix_weight], "main_four"
     )
 
 

time: 117 us -> 111 us (0.949)
  the two profiles are of different devices: /device:TPU:14 before, /device:TPU:6 now
where the time goes in v2:
time: 111 us; the launch traced here: 109 us
  Pallas kernels  90.9 us (82%)
  starting transfers between devices  9 us (8%)
  waiting for transfers between devices  8.99 us (8%)
    pallas_call x4, Pallas kernels, main(): pl.pallas_call(functools.partial(main_kernel, low=low, n_ghost=n_ghost, n...  49 us
    pallas_call x1, Pallas kernels, place(): pl.pallas_call(place_kernel, out_shape=(shape((slots, C), BF16), shape((s...  20.9 us
    pallas_call x1, Pallas kernels, body(): pl.pallas_call(radial_kernel, out_shape=(shape((tiles * TE, C), BF16), sh...  8.03 us
    pallas_call x2, Pallas kernels, pick(): pl.pallas_call(functools.partial(pick_kernel, n=n), out_shape=(shape((n,...  7.72 us
    ppermute x3, waiting for transfers between devices, body(): held = lax.ppermute(held, 'tile', ring)  5.97 us
    ppermute x2, starting transfers between devices, pick_after(): lax.ppermute(far_rows, 'dom', far)  5.11 us
    ppermute x2, waiting for transfers between devices, pick_after(): lax.ppermute(far_rows, 'dom', far)  3 us
    pallas_call x1, Pallas kernels, body(): pl.pallas_call(functools.partial(rank_kernel, slots=slots), out_shape=(sh...  2.75 us
  transfers between devices with their start and end apart: 11, of which 4 were waited for; matrix products, arithmetic and copies ran while one was open for 0% of the time, Pallas kernels for 69%

profile of v2, /device:TPU:6, one launch (start us, length us, event | category | flops | bytes accessed | tf_op | source)
XLA Modules:
  0.0 109.2 jit_solution(14949498906089105440)
XLA Ops:
  0.0 2.4 %mix.1.refs_1_.refs_0_ = bf16[1168,256]{1,0:T(8,128)(2,1)} custom-call(bf16[256,1152]{1,0:T(8,128)(2,1)} %refs_9_.3, bf16[3,256,128]{2,1,0:T(8,128)(2,1)} %refs_10_.1, s32[1,256]{1,0:T(1,128)} %bitcast.3), custom_call_target="tpu_custom_call" | custom-call | flops 75497472 | bytes 2000000 | tf_op jit(solution)/shard_map/mix/pallas_call | solution.py:438
  2.4 0.5 collective-permute-start.4
  2.9 1.6 %collective-permute-start = (bf16[1168,256]{1,0:T(8,128)(2,1)}, bf16[1168,256]{1,0:T(8,128)(2,1)}, u32[]{:S(2)}, u32[]{:S(2)}) collective-permute-start(bf16[1168,256]{1,0:T(8,128)(2,1)} %mix.1.refs_1_.refs_0_), channel_id=1, source_target_pairs={{0,2},{1,3},{2,4},{3,5},{4,6},{5,7},{6,0},{7,1},{8,10},{9,11},{10,... | collective-permute-start | bytes 1794056 | tf_op jit(solution)/shard_map/ppermute | solution.py:568
  4.5 8.0 %radial.1 = (bf16[12288,128]{1,0:T(8,128)(2,1)}, f32[256,128]{1,0:T(8,128)}) custom-call(s32[1,8]{1,0:T(1,128)} %count_ref.5, s32[96,128]{1,0:T(8,128)} %bitcast.6, bf16[12288,128]{1,0:T(8,128)(2,1)} %feat_ref.1, bf16[128,128]{1,0:T(8,128)(2,1)} %rin_ref.1), custom_call_target="tpu_custom_call" | custom-call | flops 10000000000 | bytes 6000000 | tf_op jit(solution)/shard_map/radial/pallas_call | solution.py:468
  12.5 2.8 %rank.1 = (s32[96,128]{1,0:T(8,128)}, s32[48,128]{1,0:T(8,128)}) custom-call(s32[1,8]{1,0:T(1,128)} %count_ref.5, s32[96,128]{1,0:T(8,128)} %bitcast.4), custom_call_target="tpu_custom_call" | custom-call | flops 4000000000 | bytes 1000000 | tf_op jit(solution)/shard_map/rank/pallas_call | solution.py:455
  15.3 4.8 %collective-permute-done.refs_3_.refs_2_ = bf16[1168,256]{1,0:T(8,128)(2,1)} collective-permute-done((bf16[1168,256]{1,0:T(8,128)(2,1)}, bf16[1168,256]{1,0:T(8,128)(2,1)}, u32[]{:S(2)}, u32[]{:S(2)}) %collective-permute-start) | collective-permute-done | bytes 598048 | tf_op jit(solution)/shard_map/ppermute | solution.py:568
  20.1 1.5 %collective-permute-start.5 = (bf16[1168,256]{1,0:T(8,128)(2,1)}, bf16[1168,256]{1,0:T(8,128)(2,1)}, u32[]{:S(2)}, u32[]{:S(2)}) collective-permute-start(bf16[1168,256]{1,0:T(8,128)(2,1)} %collective-permute-done.refs_3_.refs_2_), channel_id=1, source_target_pairs={{0,1},{1,0},{2,3},{3,2},{4,5},{5,4},{6,7},{7,6},{8,9},{9,8},{10,11... | collective-permute-start | bytes 1794056 | tf_op jit(solution)/shard_map/ppermute | solution.py:566
  21.6 0.0 collective-permute-start.1
  21.6 20.9 %place.1 = (bf16[16384,128]{1,0:T(8,128)(2,1)}, bf16[16384,128]{1,0:T(8,128)(2,1)}, s32[128,128]{1,0:T(8,128)}) custom-call(s32[1,8]{1,0:T(1,128)} %count_ref.5, s32[96,128]{1,0:T(8,128)} %get-tuple-element.33.pos_ref, s32[48,128]{1,0:T(8,128)} %get-tuple-element.30.span_ref.refs_0_, s32[96,128]{1,0:T(8,128)} %bitcast.5, s32[96,128]{1,0:T(8,128)} %bitcast.7, ...), custom_call_target="tpu_custom_call" | custom-call | flops 20000000000 | bytes 12000000 | tf_op jit(solution)/shard_map/place/pallas_call | solution.py:479
  42.5 0.0 collective-permute-done.1.refs_5_.refs_0_
  42.5 0.1 collective-permute-start.3
  42.6 0.1 collective-permute-start.2
  42.7 0.0 collective-permute-done.4.refs_2_.refs_1_
  42.7 0.0 collective-permute-done.5.refs_4_.refs_3_
  42.7 14.7 %main_one.1.refs_7_ = f32[1152,256]{1,0:T(8,128)} custom-call(s32[48,128]{1,0:T(8,128)} %get-tuple-element.30.span_ref.refs_0_, bf16[1168,256]{1,0:T(8,128)(2,1)} %mix.1.refs_1_.refs_0_, bf16[1168,256]{1,0:T(8,128)(2,1)} %collective-permute-done.4.refs_2_.refs_1_, bf16[1168,256]{1,0:T(8,128)(2,1)} %collective-permute-done.refs_3_.refs_2_, ...), custom_call_target="tpu_custom_call" | custom-call | flops 500000000 | bytes 500000 | tf_op jit(solution)/shard_map/main_one/pallas_call | solution.py:526
  57.4 1.2 %collective-permute-done.3.refs_2_ = bf16[1168,256]{1,0:T(8,128)(2,1)} collective-permute-done((bf16[1168,256]{1,0:T(8,128)(2,1)}, bf16[1168,256]{1,0:T(8,128)(2,1)}, u32[]{:S(2)}, u32[]{:S(2)}) %collective-permute-start.3) | collective-permute-done | bytes 598048 | tf_op jit(solution)/shard_map/ppermute | solution.py:568
  58.5 0.0 collective-permute-start.6
  58.5 3.9 %pick.2 = (bf16[4,1152,128]{2,1,0:T(8,128)(2,1)}, bf16[4,1152,128]{2,1,0:T(8,128)(2,1)}) custom-call(bf16[1168,256]{1,0:T(8,128)(2,1)} %mix.1.refs_1_.refs_0_, bf16[1168,256]{1,0:T(8,128)(2,1)} %collective-permute-done.4.refs_2_.refs_1_, bf16[1168,256]{1,0:T(8,128)(2,1)} %collective-permute-done.refs_3_.refs_2_, ...), custom_call_target="tpu_custom_call" | custom-call | flops 200000000 | bytes 400000 | tf_op jit(solution)/shard_map/pick/pallas_call | solution.py:503
  62.4 0.1 collective-permute-start.9
  62.5 3.2 %collective-permute-start.10 = (bf16[4,1152,128]{2,1,0:T(8,128)(2,1)}, bf16[4,1152,128]{2,1,0:T(8,128)(2,1)}, u32[]{:S(2)}, u32[]{:S(2)}) collective-permute-start(bf16[4,1152,128]{2,1,0:T(8,128)(2,1)} %get-tuple-element.52), channel_id=1, source_target_pairs={{8,16},{16,8},{9,17},{17,9},{10,18},{18,10},{11,19},{19,11},{12,20... | collective-permute-start | bytes 3538952 | tf_op jit(solution)/shard_map/ppermute | solution.py:581
  65.7 0.0 collective-permute-done.2.refs_1_
  65.7 8.2 %main_two.1.refs_8_ = f32[1152,256]{1,0:T(8,128)} custom-call(s32[48,128]{1,0:T(8,128)} %get-tuple-element.30.span_ref.refs_0_, bf16[1168,256]{1,0:T(8,128)(2,1)} %collective-permute-done.2.refs_1_, bf16[1168,256]{1,0:T(8,128)(2,1)} %collective-permute-done.3.refs_2_, bf16[16384,128]{1,0:T(8,128)(2,1)} %get-tuple-element.37.refs_6_.refs_3_.refs_4_, ...), custom_call_target="tpu_custom_call" | custom-call | flops 200000000 | bytes 200000 | tf_op jit(solution)/shard_map/main_two/pallas_call | solution.py:526
  73.9 0.0 collective-permute-done.6.refs_3_
  73.9 3.9 %pick.3 = (bf16[4,1152,128]{2,1,0:T(8,128)(2,1)}, bf16[4,1152,128]{2,1,0:T(8,128)(2,1)}) custom-call(bf16[1168,256]{1,0:T(8,128)(2,1)} %collective-permute-done.1.refs_5_.refs_0_, bf16[1168,256]{1,0:T(8,128)(2,1)} %collective-permute-done.2.refs_1_, bf16[1168,256]{1,0:T(8,128)(2,1)} %collective-permute-done.3.refs_2_, ...), custom_call_target="tpu_custom_call" | custom-call | flops 200000000 | bytes 400000 | tf_op jit(solution)/shard_map/pick/pallas_call | solution.py:503
  77.8 0.1 collective-permute-start.7
  77.9 1.9 %collective-permute-start.8 = (bf16[4,1152,128]{2,1,0:T(8,128)(2,1)}, bf16[4,1152,128]{2,1,0:T(8,128)(2,1)}, u32[]{:S(2)}, u32[]{:S(2)}) collective-permute-start(bf16[4,1152,128]{2,1,0:T(8,128)(2,1)} %get-tuple-element.50), channel_id=1, source_target_pairs={{8,16},{16,8},{9,17},{17,9},{10,18},{18,10},{11,19},{19,11},{12,20... | collective-permute-start | bytes 3538952 | tf_op jit(solution)/shard_map/ppermute | solution.py:581
  79.8 0.0 collective-permute-done.9.refs_1_
  79.8 0.5 collective-permute-done.10.refs_2_
  80.3 12.9 %main_three.1.refs_7_ = f32[1152,256]{1,0:T(8,128)} custom-call(s32[48,128]{1,0:T(8,128)} %get-tuple-element.30.span_ref.refs_0_, bf16[4,1152,128]{2,1,0:T(8,128)(2,1)} %collective-permute-done.9.refs_1_, bf16[4,1152,128]{2,1,0:T(8,128)(2,1)} %collective-permute-done.10.refs_2_, bf16[1168,256]{1,0:T(8,128)(2,1)} %collective-permute-done.6.refs_3_, ...), custom_call_target="tpu_custom_call" | custom-call | flops 500000000 | bytes 500000 | tf_op jit(solution)/shard_map/main_three/pallas_call | solution.py:526
  93.2 0.0 collective-permute-done.7.refs_1_
  93.2 2.5 %collective-permute-done.8.refs_2_ = bf16[4,1152,128]{2,1,0:T(8,128)(2,1)} collective-permute-done((bf16[4,1152,128]{2,1,0:T(8,128)(2,1)}, bf16[4,1152,128]{2,1,0:T(8,128)(2,1)}, u32[]{:S(2)}, u32[]{:S(2)}) %collective-permute-start.8) | collective-permute-done | bytes 1179680 | tf_op jit(solution)/shard_map/ppermute | solution.py:581
  95.7 13.3 %main_four.1 = bf16[256,1152]{1,0:T(8,128)(2,1)} custom-call(s32[48,128]{1,0:T(8,128)} %get-tuple-element.30.span_ref.refs_0_, bf16[4,1152,128]{2,1,0:T(8,128)(2,1)} %collective-permute-done.7.refs_1_, bf16[4,1152,128]{2,1,0:T(8,128)(2,1)} %collective-permute-done.8.refs_2_, bf16[16384,128]{1,0:T(8,128)(2,1)} %get-tuple-element.37.refs_6_.refs_3_.refs_4_, ...), custom_call_target="tpu_custom_call" | custom-call | flops 400000000 | bytes 400000 | tf_op jit(solution)/shard_map/main_four/pallas_call | solution.py:526
Async XLA Ops:
  2.4 40.3 %collective-permute-start.4 = (bf16[1168,256]{1,0:T(8,128)(2,1)}, bf16[1168,256]{1,0:T(8,128)(2,1)}, u32[]{:S(2)}, u32[]{:S(2)}) collective-permute-start(bf16[1168,256]{1,0:T(8,128)(2,1)} %mix.1.refs_1_.refs_0_), channel_id=1, source_target_pairs={{0,1},{1,0},{2,3},{3,2},{4,5},{5,4},{6,7},{7,6},{8,9},{9,8},{10,11... | collective-permute-start | bytes 1794056 | tf_op jit(solution)/shard_map/ppermute | solution.py:566
  2.9 17.2 %collective-permute-start = (bf16[1168,256]{1,0:T(8,128)(2,1)}, bf16[1168,256]{1,0:T(8,128)(2,1)}, u32[]{:S(2)}, u32[]{:S(2)}) collective-permute-start(bf16[1168,256]{1,0:T(8,128)(2,1)} %mix.1.refs_1_.refs_0_), channel_id=1, source_target_pairs={{0,2},{1,3},{2,4},{3,5},{4,6},{5,7},{6,0},{7,1},{8,10},{9,11},{10,... | collective-permute-start | bytes 1794056 | tf_op jit(solution)/shard_map/ppermute | solution.py:568
  20.1 22.6 %collective-permute-start.5 = (bf16[1168,256]{1,0:T(8,128)(2,1)}, bf16[1168,256]{1,0:T(8,128)(2,1)}, u32[]{:S(2)}, u32[]{:S(2)}) collective-permute-start(bf16[1168,256]{1,0:T(8,128)(2,1)} %collective-permute-done.refs_3_.refs_2_), channel_id=1, source_target_pairs={{0,1},{1,0},{2,3},{3,2},{4,5},{5,4},{6,7},{7,6},{8,9},{9,8},{10,11... | collective-permute-start | bytes 1794056 | tf_op jit(solution)/shard_map/ppermute | solution.py:566
  21.6 20.9 %collective-permute-start.1 = (bf16[1168,256]{1,0:T(8,128)(2,1)}, bf16[1168,256]{1,0:T(8,128)(2,1)}, u32[]{:S(2)}, u32[]{:S(2)}) collective-permute-start(bf16[1168,256]{1,0:T(8,128)(2,1)} %collective-permute-done.refs_3_.refs_2_), channel_id=1, source_target_pairs={{0,2},{1,3},{2,4},{3,5},{4,6},{5,7},{6,0},{7,1},{8,10},{9,11},{10,... | collective-permute-start | bytes 1794056 | tf_op jit(solution)/shard_map/ppermute | solution.py:568
  42.5 16.0 %collective-permute-start.3 = (bf16[1168,256]{1,0:T(8,128)(2,1)}, bf16[1168,256]{1,0:T(8,128)(2,1)}, u32[]{:S(2)}, u32[]{:S(2)}) collective-permute-start(bf16[1168,256]{1,0:T(8,128)(2,1)} %collective-permute-done.1.refs_5_.refs_0_), channel_id=1, source_target_pairs={{0,2},{1,3},{2,4},{3,5},{4,6},{5,7},{6,0},{7,1},{8,10},{9,11},{10,... | collective-permute-start | bytes 1794056 | tf_op jit(solution)/shard_map/ppermute | solution.py:568
  42.6 23.1 %collective-permute-start.2 = (bf16[1168,256]{1,0:T(8,128)(2,1)}, bf16[1168,256]{1,0:T(8,128)(2,1)}, u32[]{:S(2)}, u32[]{:S(2)}) collective-permute-start(bf16[1168,256]{1,0:T(8,128)(2,1)} %collective-permute-done.1.refs_5_.refs_0_), channel_id=1, source_target_pairs={{0,1},{1,0},{2,3},{3,2},{4,5},{5,4},{6,7},{7,6},{8,9},{9,8},{10,11... | collective-permute-start | bytes 1794056 | tf_op jit(solution)/shard_map/ppermute | solution.py:566
  58.5 15.4 %collective-permute-start.6 = (bf16[1168,256]{1,0:T(8,128)(2,1)}, bf16[1168,256]{1,0:T(8,128)(2,1)}, u32[]{:S(2)}, u32[]{:S(2)}) collective-permute-start(bf16[1168,256]{1,0:T(8,128)(2,1)} %collective-permute-done.3.refs_2_), channel_id=1, source_target_pairs={{0,1},{1,0},{2,3},{3,2},{4,5},{5,4},{6,7},{7,6},{8,9},{9,8},{10,11... | collective-permute-start | bytes 1794056 | tf_op jit(solution)/shard_map/ppermute | solution.py:566
  62.4 17.4 %collective-permute-start.9 = (bf16[4,1152,128]{2,1,0:T(8,128)(2,1)}, bf16[4,1152,128]{2,1,0:T(8,128)(2,1)}, u32[]{:S(2)}, u32[]{:S(2)}) collective-permute-start(bf16[4,1152,128]{2,1,0:T(8,128)(2,1)} %get-tuple-element.51), channel_id=1, source_target_pairs={{0,8},{8,0},{16,24},{24,16},{1,9},{9,1},{17,25},{25,17},{2,10},{10... | collective-permute-start | bytes 3538952 | tf_op jit(solution)/shard_map/ppermute | solution.py:581
  62.5 17.8 %collective-permute-start.10 = (bf16[4,1152,128]{2,1,0:T(8,128)(2,1)}, bf16[4,1152,128]{2,1,0:T(8,128)(2,1)}, u32[]{:S(2)}, u32[]{:S(2)}) collective-permute-start(bf16[4,1152,128]{2,1,0:T(8,128)(2,1)} %get-tuple-element.52), channel_id=1, source_target_pairs={{8,16},{16,8},{9,17},{17,9},{10,18},{18,10},{11,19},{19,11},{12,20... | collective-permute-start | bytes 3538952 | tf_op jit(solution)/shard_map/ppermute | solution.py:581
  77.8 15.4 %collective-permute-start.7 = (bf16[4,1152,128]{2,1,0:T(8,128)(2,1)}, bf16[4,1152,128]{2,1,0:T(8,128)(2,1)}, u32[]{:S(2)}, u32[]{:S(2)}) collective-permute-start(bf16[4,1152,128]{2,1,0:T(8,128)(2,1)} %get-tuple-element.49), channel_id=1, source_target_pairs={{0,8},{8,0},{16,24},{24,16},{1,9},{9,1},{17,25},{25,17},{2,10},{10... | collective-permute-start | bytes 3538952 | tf_op jit(solution)/shard_map/ppermute | solution.py:581
  77.9 17.8 %collective-permute-start.8 = (bf16[4,1152,128]{2,1,0:T(8,128)(2,1)}, bf16[4,1152,128]{2,1,0:T(8,128)(2,1)}, u32[]{:S(2)}, u32[]{:S(2)}) collective-permute-start(bf16[4,1152,128]{2,1,0:T(8,128)(2,1)} %get-tuple-element.50), channel_id=1, source_target_pairs={{8,16},{16,8},{9,17},{17,9},{10,18},{18,10},{11,19},{19,11},{12,20... | collective-permute-start | bytes 3538952 | tf_op jit(solution)/shard_map/ppermute | solution.py:581

commit v3 on v2

--- a/solution.py
+++ b/solution.py
@@ -69,8 +69,9 @@
     saves = []
     for load in loads:
         load.start()
+    for load in loads:
+        load.wait()
     for i in range(n):
-        loads[i].wait()
         picks = inside[i, WIDTH:, :].astype(F32)[:1, :].astype(I32)
         down, up = picks[:, :GHOST], picks[:, GHOST:]
         row_id = iota((ATOM_DEV, GHOST), 0)
@@ -84,12 +85,24 @@
         rows = dot(inside[i, :WIDTH, :], chosen).astype(BF16)
         near[i] = rows[:, :GHOST]
         far[i] = rows[:, GHOST:]
+    for i in range(n):
         for side, (src, dst) in enumerate(((near, near_hbm), (far, far_hbm))):
             save = pltpu.make_async_copy(src.at[i], dst.at[i], sems.at[1 + side, i])
             save.start()
             saves.append(save)
     for save in saves:
         save.wait()
+
+
+def base_kernel(rsum_ref, rout_ref, x_ref, mix_ref, base_ref, rout_t_ref):
+    rout = rout_ref[...].astype(F32)
+    rout_t_ref[...] = rout.T.astype(BF16)
+    gate_sum = jnp.dot(
+        rsum_ref[...], rout, preferred_element_type=F32, precision=lax.Precision.HIGHEST
+    )
+    for k in range(K):
+        own = dot(x_ref[:, cols(k)], mix_ref[degree_of[k], C:])
+        base_ref[cols(k), :] = (own * gate_sum[:, cols(degree_of[k])]).T
 
 
 def live_tiles(count_ref):
@@ -188,7 +201,7 @@
     span_ref,
     src_ref,
     tgt_ref,
-    rin_ref,
+    rin_hbm,
     rad_hbm,
     tgt_hbm,
     srcs_ref,
@@ -197,9 +210,18 @@
     odd,
     rad_out,
     tgt_out,
+    rin_ref,
+    rin_sems,
     sems,
 ):
     tiles = src_ref.shape[0]
+    head = min(16, tiles) * TE
+    loads = [
+        pltpu.make_async_copy(rin_hbm.at[rows, :], rin_ref.at[rows, :], rin_sems.at[i])
+        for i, rows in enumerate((pl.ds(0, head), pl.ds(head, tiles * TE - head)))
+    ]
+    for load in loads:
+        load.start()
     nb = span_ref.shape[0] // 3
     count = live_tiles(count_ref)
     flip = jnp.where((lax.axis_index("dom") & 1) == 0, GHOST, 0)
@@ -237,6 +259,7 @@
         for e in range(TE):
             pairs[pl.ds(pos_ref[t, e], 2), :] = data[2 * e : 2 * e + 2, :]
 
+    loads[0].wait()
     compute(0, even)
 
     def step(i, carry):
@@ -246,7 +269,11 @@
         scatter(2 * i + 1, odd)
         return carry
 
-    lax.fori_loop(0, (count + 1) // 2, step, 0)
+    steps = (count + 1) // 2
+    split = jnp.minimum(steps, head // (2 * TE) - 1)
+    lax.fori_loop(0, split, step, 0)
+    loads[1].wait()
+    lax.fori_loop(split, steps, step, 0)
 
     def saves(j):
         rows = pl.ds(pl.multiple_of(j * BE, BE), BE)
@@ -281,16 +308,12 @@
     lax.fori_loop(0, used, drain, 0)
 
 
-def main_kernel(*refs, low, n_ghost, n_own, first, final):
+def main_kernel(*refs, low, n_ghost, n_own, final):
     span_ref, *refs = refs
     ghosts, refs = refs[: 2 * (n_ghost > 0)], refs[2 * (n_ghost > 0) :]
     owns, refs = refs[:n_own], refs[n_own:]
-    rad_hbm, tgt_hbm, src_ref, rout_ref, *refs = refs
-    if not first:
-        part_ref, *refs = refs
-    if final:
-        rsum_ref, x_ref, mix_ref, *refs = refs
-    out_ref, rbuf, tbuf, land_ref, message_ref, tables, sems, table_sems, *refs = refs
+    rad_hbm, tgt_hbm, part_hbm, src_ref, rout_ref, *refs = refs
+    out_ref, rbuf, tbuf, land_ref, message_ref, tables, sems, table_sems, part_sem, *refs = refs
     acc_ref = refs[0] if final else out_ref
     count = n_ghost + n_own
     nb = span_ref.shape[0] // 3
@@ -308,9 +331,6 @@
     loads = [
         pltpu.make_async_copy(src, dst, table_sems.at[i]) for i, (src, dst) in enumerate(loads)
     ]
-    for load in loads:
-        load.start()
-
     def copies(p, slot):
         moves = []
         for h in range(PER):
@@ -337,11 +357,11 @@
                 copy.wait()
 
     fetch(0)
-    if first:
-        acc_ref[...] = jnp.zeros_like(acc_ref)
-    else:
-        acc_ref[...] = part_ref[...]
-    rout_t = rout_ref[...].astype(F32).T.astype(BF16)
+    for load in loads:
+        load.start()
+    part_load = pltpu.make_async_copy(part_hbm, acc_ref, part_sem)
+    part_load.start()
+    rout_t = rout_ref[...]
     atom_id = iota((BE, TE), 1).astype(F32)
     row_id = iota((CHUNK, TE), 0)
 
@@ -379,6 +399,7 @@
     arrive(0)
     fetch(1)
     gather(0)
+    part_load.wait()
 
     def step(p, carry):
         arrive(p + 1)
@@ -393,18 +414,9 @@
     def _():
         add_up()
 
-    if not final:
-        return
-    gate_sum = jnp.dot(
-        rsum_ref[...],
-        rout_ref[...].astype(F32),
-        preferred_element_type=F32,
-        precision=lax.Precision.HIGHEST,
-    )
-    for k in range(K):
-        own = dot(x_ref[:, cols(k)], mix_ref[degree_of[k], C:])
-        full = acc_ref[cols(k), :].T + own * gate_sum[:, cols(degree_of[k])]
-        out_ref[:, cols(k)] = (inv_scale * full).astype(BF16)
+    if final:
+        for k in range(K):
+            out_ref[:, cols(k)] = (inv_scale * acc_ref[cols(k), :]).T.astype(BF16)
 
 
 def shape(dims, kind):
@@ -483,7 +495,7 @@
                 shape((slots, C), BF16),
                 shape((slots // TE, TE), I32),
             ),
-            in_specs=[smem(), smem(), smem(), vmem(), vmem(), vmem()],
+            in_specs=[smem(), smem(), smem(), vmem(), vmem(), hbm],
             out_specs=(hbm, hbm, vmem()),
             scratch_shapes=[
                 pltpu.VMEM((2 * slots + 8, C), F32),
@@ -491,6 +503,8 @@
                 pltpu.VMEM((2 * TE, C), F32),
                 pltpu.VMEM((slots, C), BF16),
                 pltpu.VMEM((slots, C), BF16),
+                pltpu.VMEM((tiles * TE, C), BF16),
+                pltpu.SemaphoreType.DMA((2,)),
                 pltpu.SemaphoreType.DMA((2, slots // BE)),
             ],
             compiler_params=PARAMS,
@@ -517,25 +531,26 @@
         )(*blocks)
         return near_rows, far_rows
 
-    def main(low, ghosts, owns, part, final_args, name):
-        final = len(final_args) > 0
+    base, rout_t = pl.pallas_call(
+        base_kernel,
+        out_shape=(shape((WIDTH, ATOM_DEV), F32), shape((3 * C, C), BF16)),
+        in_specs=[vmem()] * 4,
+        out_specs=(vmem(), vmem()),
+        compiler_params=PARAMS,
+        cost_estimate=cost(1e9, 2e6),
+        name="base",
+    )(radial_sum, radial_out, embedding, mix_weight)
+
+    def main(low, ghosts, owns, part, name, final=False):
         dims, kind = ((ATOM_DEV, WIDTH), BF16) if final else ((WIDTH, ATOM_DEV), F32)
         n_ghost = half if ghosts else 0
         count_all = n_ghost + len(owns)
-        extra = [*part, *final_args]
         return pl.pallas_call(
             functools.partial(
-                main_kernel,
-                low=low,
-                n_ghost=n_ghost,
-                n_own=len(owns),
-                first=not part,
-                final=final,
+                main_kernel, low=low, n_ghost=n_ghost, n_own=len(owns), final=final
             ),
             out_shape=shape(dims, kind),
-            in_specs=[smem()]
-            + [hbm] * (len(ghosts) + len(owns) + 2)
-            + [vmem()] * (2 + len(extra)),
+            in_specs=[smem()] + [hbm] * (len(ghosts) + len(owns) + 3) + [vmem()] * 2,
             out_specs=vmem(),
             scratch_shapes=[
                 pltpu.VMEM((2, PER, BE, C), BF16),
@@ -545,12 +560,13 @@
                 pltpu.VMEM((count_all, WIDTH, ATOM_DEV), BF16),
                 pltpu.SemaphoreType.DMA((2, PER, 2)),
                 pltpu.SemaphoreType.DMA((2 * n_ghost + len(owns),)),
+                pltpu.SemaphoreType.DMA,
             ]
             + ([pltpu.VMEM((WIDTH, ATOM_DEV), F32)] if final else []),
             compiler_params=PARAMS,
             cost_estimate=cost(1e8 * count_all, 1e5 * count_all),
             name=name,
-        )(span, *ghosts, *owns, radial_sorted, target_sorted, source_sorted, radial_out, *extra)
+        )(span, *ghosts, *owns, radial_sorted, target_sorted, part, source_sorted, rout_t)
 
     together = lax.optimization_barrier
     ring_rows, flip_rows = [mixed], []
@@ -560,14 +576,15 @@
         if k == n_ring - 1:
             early = [rows for pair in zip(ring_rows, flip_rows) for rows in pair]
             early.append(ring_rows[half // 2])
-            part = main(0, [], early[: half + 1], [], [], "main_one")
+            part = main(0, [], early[: half + 1], base, "main_one")
             held, part = together((held, part))
             ring_rows[-1] = held
-        flip_rows.append(lax.ppermute(held, "tile", flip))
+        swap = together((held, span))[0] if k == 0 else held
+        flip_rows.append(lax.ppermute(swap, "tile", flip))
         if k < n_ring - 1:
             held = lax.ppermute(held, "tile", ring)
             if k == 0:
-                held, radial = together((held, radial))
+                held, radial, base = together((held, radial, base))
                 radial_sorted, target_sorted, source_sorted = place(radial)
             if k == 1:
                 held, radial_sorted = together((held, radial_sorted))
@@ -581,12 +598,10 @@
         return [lax.ppermute(near_rows, "dom", near), lax.ppermute(far_rows, "dom", far)], part
 
     ghosts_a, part = pick_after(owns[:half], part)
-    part = main(half + 1, [], owns[half + 1 : -1], [part], [], "main_two")
+    part = main(half + 1, [], owns[half + 1 : -1], part, "main_two")
     ghosts_b, part = pick_after(owns[half:], part)
-    part = main(n_tile - 1, ghosts_a, owns[-1:], [part], [], "main_three")
-    return main(
-        n_tile + half, ghosts_b, [], [part], [radial_sum, embedding, mix_weight], "main_four"
-    )
+    part = main(n_tile - 1, ghosts_a, owns[-1:], part, "main_three")
+    return main(n_tile + half, ghosts_b, [], part, "main_four", final=True)
 
 
 def solution(mesh):

time: 111 us -> 110 us (level)
  the two profiles are of different devices: /device:TPU:6 before, /device:TPU:9 now
where the time goes in v3:
time: 110 us
  Pallas kernels  93.1 us (85%)
  starting transfers between devices  15.4 us (14%)
  waiting for transfers between devices  1.31 us (1%)
    pallas_call x4, Pallas kernels, main(): pl.pallas_call(functools.partial(main_kernel, low=low, n_ghost=n_ghost, n...  47.7 us
    pallas_call x1, Pallas kernels, place(): pl.pallas_call(place_kernel, out_shape=(shape((slots, C), BF16), shape((s...  21.2 us
    pallas_call x1, Pallas kernels, body(): pl.pallas_call(radial_kernel, out_shape=(shape((tiles * TE, C), BF16), sh...  7.97 us
    pallas_call x2, Pallas kernels, pick(): pl.pallas_call(functools.partial(pick_kernel, n=n), out_shape=(shape((n,...  7.88 us
    ppermute x2, starting transfers between devices, pick_after(): lax.ppermute(far_rows, 'dom', far)  7.71 us
    ppermute x2, starting transfers between devices, pick_after(): lax.ppermute(near_rows, 'dom', near)  4.26 us
    pallas_call x1, Pallas kernels, body(): pl.pallas_call(base_kernel, out_shape=(shape((WIDTH, ATOM_DEV), F32), sha...  3.18 us
    pallas_call x1, Pallas kernels, body(): pl.pallas_call(functools.partial(rank_kernel, slots=slots), out_shape=(sh...  2.76 us
  transfers between devices with their start and end apart: 11, of which 3 were waited for; matrix products, arithmetic and copies ran while one was open for 0% of the time, Pallas kernels for 71%

profile of v3, /device:TPU:9, one launch (start us, length us, event | category | flops | bytes accessed | tf_op | source)
XLA Modules:
  0.0 110.1 jit_solution(5815232364705922208)
XLA Ops:
  0.0 2.4 %mix.1.refs_1_.refs_0_ = bf16[1168,256]{1,0:T(8,128)(2,1)} custom-call(bf16[256,1152]{1,0:T(8,128)(2,1)} %x_ref.3, bf16[3,256,128]{2,1,0:T(8,128)(2,1)} %mix_ref.3, s32[1,256]{1,0:T(1,128)} %bitcast.3), custom_call_target="tpu_custom_call" | custom-call | flops 75497472 | bytes 2000000 | tf_op jit(solution)/shard_map/mix/pallas_call | solution.py:450
  2.4 1.3 %collective-permute-start = (bf16[1168,256]{1,0:T(8,128)(2,1)}, bf16[1168,256]{1,0:T(8,128)(2,1)}, u32[]{:S(2)}, u32[]{:S(2)}) collective-permute-start(bf16[1168,256]{1,0:T(8,128)(2,1)} %mix.1.refs_1_.refs_0_), channel_id=1, source_target_pairs={{0,2},{1,3},{2,4},{3,5},{4,6},{5,7},{6,0},{7,1},{8,10},{9,11},{10,... | collective-permute-start | bytes 1794056 | tf_op jit(solution)/shard_map/ppermute | solution.py:585
  3.7 2.8 %rank.1 = (s32[96,128]{1,0:T(8,128)}, s32[48,128]{1,0:T(8,128)}) custom-call(s32[1,8]{1,0:T(1,128)} %count_ref.5, s32[96,128]{1,0:T(8,128)} %bitcast.4), custom_call_target="tpu_custom_call" | custom-call | flops 4000000000 | bytes 1000000 | tf_op jit(solution)/shard_map/rank/pallas_call | solution.py:467
  6.5 1.2 %collective-permute-start.4 = (bf16[1168,256]{1,0:T(8,128)(2,1)}, bf16[1168,256]{1,0:T(8,128)(2,1)}, u32[]{:S(2)}, u32[]{:S(2)}) collective-permute-start(bf16[1168,256]{1,0:T(8,128)(2,1)} %mix.1.refs_1_.refs_0_), channel_id=1, source_target_pairs={{0,1},{1,0},{2,3},{3,2},{4,5},{5,4},{6,7},{7,6},{8,9},{9,8},{10,11... | collective-permute-start | bytes 1794056 | tf_op jit(solution)/shard_map/ppermute | solution.py:583
  7.7 8.0 %radial.1 = (bf16[12288,128]{1,0:T(8,128)(2,1)}, f32[256,128]{1,0:T(8,128)}) custom-call(s32[1,8]{1,0:T(1,128)} %count_ref.5, s32[96,128]{1,0:T(8,128)} %bitcast.6, bf16[12288,128]{1,0:T(8,128)(2,1)} %feat_ref.1, bf16[128,128]{1,0:T(8,128)(2,1)} %rin_ref.1), custom_call_target="tpu_custom_call" | custom-call | flops 10000000000 | bytes 6000000 | tf_op jit(solution)/shard_map/radial/pallas_call | solution.py:480
  15.7 3.2 %base.1 = (f32[1152,256]{1,0:T(8,128)}, bf16[384,128]{1,0:T(8,128)(2,1)}) custom-call(f32[256,128]{1,0:T(8,128)} %get-tuple-element.36.rsum_ref, bf16[128,384]{1,0:T(8,128)(2,1)} %rout_ref.1, bf16[256,1152]{1,0:T(8,128)(2,1)} %x_ref.3, bf16[3,256,128]{2,1,0:T(8,128)(2,1)} %mix_ref.3), custom_call_target="tpu_custom_call" | custom-call | flops 1000000000 | bytes 2000000 | tf_op jit(solution)/shard_map/base/pallas_call | solution.py:534
  18.9 0.0 collective-permute-done.refs_3_.refs_2_
  18.9 0.0 collective-permute-start.5
  18.9 0.8 collective-permute-start.1
  19.6 21.2 %place.1 = (bf16[16384,128]{1,0:T(8,128)(2,1)}, bf16[16384,128]{1,0:T(8,128)(2,1)}, s32[128,128]{1,0:T(8,128)}) custom-call(s32[1,8]{1,0:T(1,128)} %count_ref.5, s32[96,128]{1,0:T(8,128)} %get-tuple-element.39.pos_ref, s32[48,128]{1,0:T(8,128)} %get-tuple-element.34.span_ref.refs_0_, s32[96,128]{1,0:T(8,128)} %bitcast.5, s32[96,128]{1,0:T(8,128)} %bitcast.7, ...), custom_call_target="tpu_custom_call" | custom-call | flops 20000000000 | bytes 12000000 | tf_op jit(solution)/shard_map/place/pallas_call | solution.py:491
  40.8 0.0 collective-permute-done.1.refs_5_.refs_0_
  40.8 0.1 collective-permute-start.3
  40.9 0.1 collective-permute-start.2
  41.0 0.0 collective-permute-done.4.refs_2_.refs_1_
  41.0 0.0 collective-permute-done.5.refs_4_.refs_3_
  41.0 12.6 %main_one.1.refs_5_ = f32[1152,256]{1,0:T(8,128)} custom-call(s32[48,128]{1,0:T(8,128)} %get-tuple-element.34.span_ref.refs_0_, bf16[1168,256]{1,0:T(8,128)(2,1)} %mix.1.refs_1_.refs_0_, bf16[1168,256]{1,0:T(8,128)(2,1)} %collective-permute-done.4.refs_2_.refs_1_, bf16[1168,256]{1,0:T(8,128)(2,1)} %collective-permute-done.refs_3_.refs_2_, ...), custom_call_target="tpu_custom_call" | custom-call | flops 500000000 | bytes 500000 | tf_op jit(solution)/shard_map/main_one/pallas_call | solution.py:548
  53.6 0.4 collective-permute-done.3.refs_2_
  54.0 0.0 collective-permute-start.6
  54.0 4.0 %pick.2 = (bf16[4,1152,128]{2,1,0:T(8,128)(2,1)}, bf16[4,1152,128]{2,1,0:T(8,128)(2,1)}) custom-call(bf16[1168,256]{1,0:T(8,128)(2,1)} %mix.1.refs_1_.refs_0_, bf16[1168,256]{1,0:T(8,128)(2,1)} %collective-permute-done.4.refs_2_.refs_1_, bf16[1168,256]{1,0:T(8,128)(2,1)} %collective-permute-done.refs_3_.refs_2_, ...), custom_call_target="tpu_custom_call" | custom-call | flops 200000000 | bytes 400000 | tf_op jit(solution)/shard_map/pick/pallas_call | solution.py:517
  57.9 4.2 %collective-permute-start.9 = (bf16[4,1152,128]{2,1,0:T(8,128)(2,1)}, bf16[4,1152,128]{2,1,0:T(8,128)(2,1)}, u32[]{:S(2)}, u32[]{:S(2)}) collective-permute-start(bf16[4,1152,128]{2,1,0:T(8,128)(2,1)} %get-tuple-element.60), channel_id=1, source_target_pairs={{0,8},{8,0},{16,24},{24,16},{1,9},{9,1},{17,25},{25,17},{2,10},{10... | collective-permute-start | bytes 3538952 | tf_op jit(solution)/shard_map/ppermute | solution.py:598
  62.1 5.6 %collective-permute-start.10 = (bf16[4,1152,128]{2,1,0:T(8,128)(2,1)}, bf16[4,1152,128]{2,1,0:T(8,128)(2,1)}, u32[]{:S(2)}, u32[]{:S(2)}) collective-permute-start(bf16[4,1152,128]{2,1,0:T(8,128)(2,1)} %get-tuple-element.61), channel_id=1, source_target_pairs={{8,16},{16,8},{9,17},{17,9},{10,18},{18,10},{11,19},{19,11},{12,20... | collective-permute-start | bytes 3538952 | tf_op jit(solution)/shard_map/ppermute | solution.py:598
  67.7 0.0 collective-permute-done.2.refs_1_
  67.7 7.9 %main_two.1.refs_6_ = f32[1152,256]{1,0:T(8,128)} custom-call(s32[48,128]{1,0:T(8,128)} %get-tuple-element.34.span_ref.refs_0_, bf16[1168,256]{1,0:T(8,128)(2,1)} %collective-permute-done.2.refs_1_, bf16[1168,256]{1,0:T(8,128)(2,1)} %collective-permute-done.3.refs_2_, bf16[16384,128]{1,0:T(8,128)(2,1)} %get-tuple-element.44.refs_6_.refs_3_.refs_4_, ...), custom_call_target="tpu_custom_call" | custom-call | flops 200000000 | bytes 200000 | tf_op jit(solution)/shard_map/main_two/pallas_call | solution.py:548
  75.6 0.0 collective-permute-done.6.refs_3_
  75.6 3.9 %pick.3 = (bf16[4,1152,128]{2,1,0:T(8,128)(2,1)}, bf16[4,1152,128]{2,1,0:T(8,128)(2,1)}) custom-call(bf16[1168,256]{1,0:T(8,128)(2,1)} %collective-permute-done.1.refs_5_.refs_0_, bf16[1168,256]{1,0:T(8,128)(2,1)} %collective-permute-done.2.refs_1_, bf16[1168,256]{1,0:T(8,128)(2,1)} %collective-permute-done.3.refs_2_, ...), custom_call_target="tpu_custom_call" | custom-call | flops 200000000 | bytes 400000 | tf_op jit(solution)/shard_map/pick/pallas_call | solution.py:517
  79.6 0.1 collective-permute-start.7
  79.6 2.1 %collective-permute-start.8 = (bf16[4,1152,128]{2,1,0:T(8,128)(2,1)}, bf16[4,1152,128]{2,1,0:T(8,128)(2,1)}, u32[]{:S(2)}, u32[]{:S(2)}) collective-permute-start(bf16[4,1152,128]{2,1,0:T(8,128)(2,1)} %get-tuple-element.59), channel_id=1, source_target_pairs={{8,16},{16,8},{9,17},{17,9},{10,18},{18,10},{11,19},{19,11},{12,20... | collective-permute-start | bytes 3538952 | tf_op jit(solution)/shard_map/ppermute | solution.py:598
  81.8 0.0 collective-permute-done.9.refs_1_
  81.8 0.1 collective-permute-done.10.refs_2_
  81.9 14.7 %main_three.1.refs_5_ = f32[1152,256]{1,0:T(8,128)} custom-call(s32[48,128]{1,0:T(8,128)} %get-tuple-element.34.span_ref.refs_0_, bf16[4,1152,128]{2,1,0:T(8,128)(2,1)} %collective-permute-done.9.refs_1_, bf16[4,1152,128]{2,1,0:T(8,128)(2,1)} %collective-permute-done.10.refs_2_, bf16[1168,256]{1,0:T(8,128)(2,1)} %collective-permute-done.6.refs_3_, ...), custom_call_target="tpu_custom_call" | custom-call | flops 500000000 | bytes 500000 | tf_op jit(solution)/shard_map/main_three/pallas_call | solution.py:548
  96.6 0.8 collective-permute-done.8.refs_2_
  97.5 12.4 %main_four.1 = bf16[256,1152]{1,0:T(8,128)(2,1)} custom-call(s32[48,128]{1,0:T(8,128)} %get-tuple-element.34.span_ref.refs_0_, bf16[4,1152,128]{2,1,0:T(8,128)(2,1)} %collective-permute-done.7.refs_1_, bf16[4,1152,128]{2,1,0:T(8,128)(2,1)} %collective-permute-done.8.refs_2_, bf16[16384,128]{1,0:T(8,128)(2,1)} %get-tuple-element.44.refs_6_.refs_3_.refs_4_, ...), custom_call_target="tpu_custom_call" | custom-call | flops 400000000 | bytes 400000 | tf_op jit(solution)/shard_map/main_four/pallas_call | solution.py:548
  (1 shorter events, 0.0 us)
Async XLA Ops:
  2.4 16.4 %collective-permute-start = (bf16[1168,256]{1,0:T(8,128)(2,1)}, bf16[1168,256]{1,0:T(8,128)(2,1)}, u32[]{:S(2)}, u32[]{:S(2)}) collective-permute-start(bf16[1168,256]{1,0:T(8,128)(2,1)} %mix.1.refs_1_.refs_0_), channel_id=1, source_target_pairs={{0,2},{1,3},{2,4},{3,5},{4,6},{5,7},{6,0},{7,1},{8,10},{9,11},{10,... | collective-permute-start | bytes 1794056 | tf_op jit(solution)/shard_map/ppermute | solution.py:585
  6.5 34.5 %collective-permute-start.4 = (bf16[1168,256]{1,0:T(8,128)(2,1)}, bf16[1168,256]{1,0:T(8,128)(2,1)}, u32[]{:S(2)}, u32[]{:S(2)}) collective-permute-start(bf16[1168,256]{1,0:T(8,128)(2,1)} %mix.1.refs_1_.refs_0_), channel_id=1, source_target_pairs={{0,1},{1,0},{2,3},{3,2},{4,5},{5,4},{6,7},{7,6},{8,9},{9,8},{10,11... | collective-permute-start | bytes 1794056 | tf_op jit(solution)/shard_map/ppermute | solution.py:583
  18.9 22.1 %collective-permute-start.5 = (bf16[1168,256]{1,0:T(8,128)(2,1)}, bf16[1168,256]{1,0:T(8,128)(2,1)}, u32[]{:S(2)}, u32[]{:S(2)}) collective-permute-start(bf16[1168,256]{1,0:T(8,128)(2,1)} %collective-permute-done.refs_3_.refs_2_), channel_id=1, source_target_pairs={{0,1},{1,0},{2,3},{3,2},{4,5},{5,4},{6,7},{7,6},{8,9},{9,8},{10,11... | collective-permute-start | bytes 1794056 | tf_op jit(solution)/shard_map/ppermute | solution.py:583
  18.9 21.9 %collective-permute-start.1 = (bf16[1168,256]{1,0:T(8,128)(2,1)}, bf16[1168,256]{1,0:T(8,128)(2,1)}, u32[]{:S(2)}, u32[]{:S(2)}) collective-permute-start(bf16[1168,256]{1,0:T(8,128)(2,1)} %collective-permute-done.refs_3_.refs_2_), channel_id=1, source_target_pairs={{0,2},{1,3},{2,4},{3,5},{4,6},{5,7},{6,0},{7,1},{8,10},{9,11},{10,... | collective-permute-start | bytes 1794056 | tf_op jit(solution)/shard_map/ppermute | solution.py:585
  40.8 13.1 %collective-permute-start.3 = (bf16[1168,256]{1,0:T(8,128)(2,1)}, bf16[1168,256]{1,0:T(8,128)(2,1)}, u32[]{:S(2)}, u32[]{:S(2)}) collective-permute-start(bf16[1168,256]{1,0:T(8,128)(2,1)} %collective-permute-done.1.refs_5_.refs_0_), channel_id=1, source_target_pairs={{0,2},{1,3},{2,4},{3,5},{4,6},{5,7},{6,0},{7,1},{8,10},{9,11},{10,... | collective-permute-start | bytes 1794056 | tf_op jit(solution)/shard_map/ppermute | solution.py:585
  40.9 26.8 %collective-permute-start.2 = (bf16[1168,256]{1,0:T(8,128)(2,1)}, bf16[1168,256]{1,0:T(8,128)(2,1)}, u32[]{:S(2)}, u32[]{:S(2)}) collective-permute-start(bf16[1168,256]{1,0:T(8,128)(2,1)} %collective-permute-done.1.refs_5_.refs_0_), channel_id=1, source_target_pairs={{0,1},{1,0},{2,3},{3,2},{4,5},{5,4},{6,7},{7,6},{8,9},{9,8},{10,11... | collective-permute-start | bytes 1794056 | tf_op jit(solution)/shard_map/ppermute | solution.py:583
  54.0 21.7 %collective-permute-start.6 = (bf16[1168,256]{1,0:T(8,128)(2,1)}, bf16[1168,256]{1,0:T(8,128)(2,1)}, u32[]{:S(2)}, u32[]{:S(2)}) collective-permute-start(bf16[1168,256]{1,0:T(8,128)(2,1)} %collective-permute-done.3.refs_2_), channel_id=1, source_target_pairs={{0,1},{1,0},{2,3},{3,2},{4,5},{5,4},{6,7},{7,6},{8,9},{9,8},{10,11... | collective-permute-start | bytes 1794056 | tf_op jit(solution)/shard_map/ppermute | solution.py:583
  57.9 23.9 %collective-permute-start.9 = (bf16[4,1152,128]{2,1,0:T(8,128)(2,1)}, bf16[4,1152,128]{2,1,0:T(8,128)(2,1)}, u32[]{:S(2)}, u32[]{:S(2)}) collective-permute-start(bf16[4,1152,128]{2,1,0:T(8,128)(2,1)} %get-tuple-element.60), channel_id=1, source_target_pairs={{0,8},{8,0},{16,24},{24,16},{1,9},{9,1},{17,25},{25,17},{2,10},{10... | collective-permute-start | bytes 3538952 | tf_op jit(solution)/shard_map/ppermute | solution.py:598
  62.1 19.8 %collective-permute-start.10 = (bf16[4,1152,128]{2,1,0:T(8,128)(2,1)}, bf16[4,1152,128]{2,1,0:T(8,128)(2,1)}, u32[]{:S(2)}, u32[]{:S(2)}) collective-permute-start(bf16[4,1152,128]{2,1,0:T(8,128)(2,1)} %get-tuple-element.61), channel_id=1, source_target_pairs={{8,16},{16,8},{9,17},{17,9},{10,18},{18,10},{11,19},{19,11},{12,20... | collective-permute-start | bytes 3538952 | tf_op jit(solution)/shard_map/ppermute | solution.py:598
  79.6 17.1 %collective-permute-start.7 = (bf16[4,1152,128]{2,1,0:T(8,128)(2,1)}, bf16[4,1152,128]{2,1,0:T(8,128)(2,1)}, u32[]{:S(2)}, u32[]{:S(2)}) collective-permute-start(bf16[4,1152,128]{2,1,0:T(8,128)(2,1)} %get-tuple-element.58), channel_id=1, source_target_pairs={{0,8},{8,0},{16,24},{24,16},{1,9},{9,1},{17,25},{25,17},{2,10},{10... | collective-permute-start | bytes 3538952 | tf_op jit(solution)/shard_map/ppermute | solution.py:598
  79.6 17.8 %collective-permute-start.8 = (bf16[4,1152,128]{2,1,0:T(8,128)(2,1)}, bf16[4,1152,128]{2,1,0:T(8,128)(2,1)}, u32[]{:S(2)}, u32[]{:S(2)}) collective-permute-start(bf16[4,1152,128]{2,1,0:T(8,128)(2,1)} %get-tuple-element.59), channel_id=1, source_target_pairs={{8,16},{16,8},{9,17},{17,9},{10,18},{18,10},{11,19},{19,11},{12,20... | collective-permute-start | bytes 3538952 | tf_op jit(solution)/shard_map/ppermute | solution.py:598

commit v4 on v3

--- a/solution.py
+++ b/solution.py
@@ -59,10 +59,26 @@
     mixed_ref[WIDTH:, :] = picks.astype(BF16)
 
 
+def pick_rows(table, picks, near_ref, far_ref):
+    even = (lax.axis_index("dom") & 1) == 0
+    picks = picks.astype(F32)[:1, :].astype(I32)
+    down, up = picks[:, :GHOST], picks[:, GHOST:]
+    row_id = iota((ATOM_DEV, GHOST), 0)
+    chosen = jnp.concatenate(
+        [
+            as_bf16(row_id == jnp.where(even, up, down)),
+            as_bf16(row_id == jnp.where(even, down, up)),
+        ],
+        axis=1,
+    )
+    rows = dot(table, chosen).astype(BF16)
+    near_ref[...] = rows[:, :GHOST]
+    far_ref[...] = rows[:, GHOST:]
+
+
 def pick_kernel(*refs, n):
     blocks, refs = refs[:n], refs[n:]
     near_hbm, far_hbm, inside, near, far, sems = refs
-    even = (lax.axis_index("dom") & 1) == 0
     loads = [
         pltpu.make_async_copy(block, inside.at[i], sems.at[0, i]) for i, block in enumerate(blocks)
     ]
@@ -72,19 +88,7 @@
     for load in loads:
         load.wait()
     for i in range(n):
-        picks = inside[i, WIDTH:, :].astype(F32)[:1, :].astype(I32)
-        down, up = picks[:, :GHOST], picks[:, GHOST:]
-        row_id = iota((ATOM_DEV, GHOST), 0)
-        chosen = jnp.concatenate(
-            [
-                as_bf16(row_id == jnp.where(even, up, down)),
-                as_bf16(row_id == jnp.where(even, down, up)),
-            ],
-            axis=1,
-        )
-        rows = dot(inside[i, :WIDTH, :], chosen).astype(BF16)
-        near[i] = rows[:, :GHOST]
-        far[i] = rows[:, GHOST:]
+        pick_rows(inside[i, :WIDTH, :], inside[i, WIDTH:, :], near.at[i], far.at[i])
     for i in range(n):
         for side, (src, dst) in enumerate(((near, near_hbm), (far, far_hbm))):
             save = pltpu.make_async_copy(src.at[i], dst.at[i], sems.at[1 + side, i])
@@ -113,15 +117,20 @@
     tiles = src_ref.shape[0]
     nb = span_ref.shape[0] // 3
     count = live_tiles(count_ref)
-    owns, half = nb // 2, nb // 4
+    half, few = nb // 4, nb // 8
     order = iota((nb, TE), 0)
-    ghost = ((order >= owns - 1) & (order < owns - 1 + half)) | (order >= owns + half)
-    index = jnp.where(order >= owns - 1, order - (owns - 1), order)
-    index = jnp.where(order == owns - 1 + half, owns - 1, index)
-    index = jnp.where(order >= owns + half, order - owns, index)
+    ghost = ((order >= half + few) & (order < 2 * half + few)) | (order >= 3 * half)
+    index = order
+    index = jnp.where(order >= half, half + 2 * (order - half), index)
+    index = jnp.where(order >= half + few, order - (half + few), index)
+    index = jnp.where(order >= 2 * half + few, half + 2 * (order - (2 * half + few)) + 1, index)
+    index = jnp.where(order >= 3 * half, order - 2 * half, index)
     tile_pos = lax.axis_index("tile")
-    ring_pos = (tile_pos >> 1) - (index >> 1)
+    step = index >> 1
+    ahead = half // 2
+    ring_pos = (tile_pos >> 1) + jnp.where(step <= ahead, -step, step - ahead)
     ring_pos = jnp.where(ring_pos < 0, ring_pos + half, ring_pos)
+    ring_pos = jnp.where(ring_pos >= half, ring_pos - half, ring_pos)
     label = 2 * (2 * ring_pos + ((tile_pos & 1) ^ (index & 1))) + jnp.where(ghost, 1, 0)
 
     def mark(t, carry):
@@ -308,13 +317,18 @@
     lax.fori_loop(0, used, drain, 0)
 
 
-def main_kernel(*refs, low, n_ghost, n_own, final):
+def main_kernel(*refs, low, n_ghost, n_own, n_pick, final):
     span_ref, *refs = refs
     ghosts, refs = refs[: 2 * (n_ghost > 0)], refs[2 * (n_ghost > 0) :]
     owns, refs = refs[:n_own], refs[n_own:]
     rad_hbm, tgt_hbm, part_hbm, src_ref, rout_ref, *refs = refs
-    out_ref, rbuf, tbuf, land_ref, message_ref, tables, sems, table_sems, part_sem, *refs = refs
+    out_ref, *refs = refs
+    if n_pick:
+        near_hbm, far_hbm, *refs = refs
+    rbuf, tbuf, land_ref, message_ref, tables, sems, table_sems, part_sem, *refs = refs
     acc_ref = refs[0] if final else out_ref
+    if n_pick:
+        picks, near, far, pick_sems = refs
     count = n_ghost + n_own
     nb = span_ref.shape[0] // 3
     begin = span_ref[low, 0]
@@ -331,6 +345,9 @@
     loads = [
         pltpu.make_async_copy(src, dst, table_sems.at[i]) for i, (src, dst) in enumerate(loads)
     ]
+    for i in range(n_pick):
+        load = pltpu.make_async_copy(owns[i].at[WIDTH:, :], picks.at[i], pick_sems.at[0, i])
+        loads.append(load)
     def copies(p, slot):
         moves = []
         for h in range(PER):
@@ -396,6 +413,14 @@
 
     for load in loads:
         load.wait()
+    saves = []
+    for i in range(n_pick):
+        pick_rows(tables[i], picks[i], near.at[i], far.at[i])
+    for i in range(n_pick):
+        for side, (src, dst) in enumerate(((near, near_hbm), (far, far_hbm))):
+            save = pltpu.make_async_copy(src.at[i], dst.at[i], pick_sems.at[1 + side, i])
+            save.start()
+            saves.append(save)
     arrive(0)
     fetch(1)
     gather(0)
@@ -414,6 +439,8 @@
     def _():
         add_up()
 
+    for save in saves:
+        save.wait()
     if final:
         for k in range(K):
             out_ref[:, cols(k)] = (inv_scale * acc_ref[cols(k), :]).T.astype(BF16)
@@ -457,6 +484,7 @@
         name="mix",
     )(embedding, mix_weight, ghost_index.reshape(1, ATOM_DEV))
     ring = [(t, (t + 2) % n_tile) for t in range(n_tile)]
+    back = [(target, source) for source, target in ring]
     flip = [(t, t ^ 1) for t in range(n_tile)]
     near = [(i, i ^ 1) for i in range(n_dom)]
     far = [(i, i + 1) for i in range(1, n_dom - 1, 2)]
@@ -541,17 +569,23 @@
         name="base",
     )(radial_sum, radial_out, embedding, mix_weight)
 
-    def main(low, ghosts, owns, part, name, final=False):
+    def main(low, ghosts, owns, part, name, n_pick=0, final=False):
         dims, kind = ((ATOM_DEV, WIDTH), BF16) if final else ((WIDTH, ATOM_DEV), F32)
         n_ghost = half if ghosts else 0
         count_all = n_ghost + len(owns)
         return pl.pallas_call(
             functools.partial(
-                main_kernel, low=low, n_ghost=n_ghost, n_own=len(owns), final=final
+                main_kernel,
+                low=low,
+                n_ghost=n_ghost,
+                n_own=len(owns),
+                n_pick=n_pick,
+                final=final,
             ),
-            out_shape=shape(dims, kind),
+            out_shape=(shape(dims, kind),)
+            + ((shape((n_pick, WIDTH, GHOST), BF16),) * 2 if n_pick else ()),
             in_specs=[smem()] + [hbm] * (len(ghosts) + len(owns) + 3) + [vmem()] * 2,
-            out_specs=vmem(),
+            out_specs=(vmem(),) + ((hbm, hbm) if n_pick else ()),
             scratch_shapes=[
                 pltpu.VMEM((2, PER, BE, C), BF16),
                 pltpu.VMEM((2, PER, BE, C), BF16),
@@ -562,46 +596,58 @@
                 pltpu.SemaphoreType.DMA((2 * n_ghost + len(owns),)),
                 pltpu.SemaphoreType.DMA,
             ]
-            + ([pltpu.VMEM((WIDTH, ATOM_DEV), F32)] if final else []),
+            + ([pltpu.VMEM((WIDTH, ATOM_DEV), F32)] if final else [])
+            + (
+                [
+                    pltpu.VMEM((n_pick, EXTRA, ATOM_DEV), BF16),
+                    pltpu.VMEM((n_pick, WIDTH, GHOST), BF16),
+                    pltpu.VMEM((n_pick, WIDTH, GHOST), BF16),
+                    pltpu.SemaphoreType.DMA((3, n_pick)),
+                ]
+                if n_pick
+                else []
+            ),
             compiler_params=PARAMS,
             cost_estimate=cost(1e8 * count_all, 1e5 * count_all),
             name=name,
         )(span, *ghosts, *owns, radial_sorted, target_sorted, part, source_sorted, rout_t)
 
     together = lax.optimization_barrier
-    ring_rows, flip_rows = [mixed], []
-    held = mixed
-    part = None
-    for k in range(n_ring):
-        if k == n_ring - 1:
-            early = [rows for pair in zip(ring_rows, flip_rows) for rows in pair]
-            early.append(ring_rows[half // 2])
-            part = main(0, [], early[: half + 1], base, "main_one")
-            held, part = together((held, part))
-            ring_rows[-1] = held
-        swap = together((held, span))[0] if k == 0 else held
-        flip_rows.append(lax.ppermute(swap, "tile", flip))
-        if k < n_ring - 1:
-            held = lax.ppermute(held, "tile", ring)
-            if k == 0:
-                held, radial, base = together((held, radial, base))
-                radial_sorted, target_sorted, source_sorted = place(radial)
-            if k == 1:
-                held, radial_sorted = together((held, radial_sorted))
-            ring_rows.append(held)
-    owns = [rows for pair in zip(ring_rows, flip_rows) for rows in pair]
-
-    def pick_after(blocks, part):
-        first, part = together((blocks[0], part))
-        near_rows, far_rows = pick([first, *blocks[1:]])
-        near_rows, part = together((near_rows, part))
-        return [lax.ppermute(near_rows, "dom", near), lax.ppermute(far_rows, "dom", far)], part
-
-    ghosts_a, part = pick_after(owns[:half], part)
-    part = main(half + 1, [], owns[half + 1 : -1], part, "main_two")
-    ghosts_b, part = pick_after(owns[half:], part)
-    part = main(n_tile - 1, ghosts_a, owns[-1:], part, "main_three")
-    return main(n_tile + half, ghosts_b, [], part, "main_four", final=True)
+
+    def to_ring(rows):
+        return lax.ppermute(rows, "tile", ring)
+
+    def to_flip(rows):
+        return lax.ppermute(rows, "tile", flip)
+
+    def exchange(near_rows, far_rows):
+        return [lax.ppermute(near_rows, "dom", near), lax.ppermute(far_rows, "dom", far)]
+
+    few = half // 2
+    ahead = [mixed, to_ring(mixed)]
+    behind = [lax.ppermute(together((mixed, radial))[0], "tile", back)]
+    ahead[1], radial, base = together((ahead[1], radial, base))
+    flips = [to_flip(together((mixed, span))[0]), to_flip(ahead[1])]
+    while len(ahead) <= few:
+        ahead.append(to_ring(ahead[-1]))
+    while len(behind) < n_ring - 1 - few:
+        behind.append(lax.ppermute(behind[-1], "tile", back))
+    radial_sorted, target_sorted, source_sorted = place(radial)
+    ahead[2], behind[0], radial_sorted = together((ahead[2], behind[0], radial_sorted))
+    rings = ahead + behind
+    flips += [to_flip(rows) for rows in rings[2:]]
+    owns = [rows for pair in zip(rings, flips) for rows in pair]
+    part, near_rows, far_rows = main(
+        0, [], owns[:half] + rings[few:], base, "main_one", n_pick=half
+    )
+    ghosts_a = exchange(near_rows, far_rows)
+    last = owns[half:]
+    last[0], part = together((last[0], part))
+    near_rows, far_rows = pick(last)
+    near_rows, part = together((near_rows, part))
+    ghosts_b = exchange(near_rows, far_rows)
+    (part,) = main(half + few, ghosts_a, flips[few:], part, "main_two")
+    return main(n_tile + half, ghosts_b, [], part, "main_three", final=True)[0]
 
 
 def solution(mesh):

time: 110 us -> 121 us (1.10)
  the two profiles are of different devices: /device:TPU:9 before, /device:TPU:10 now
where the time goes in v4:
time: 121 us; the launch traced here: 119 us
  Pallas kernels  86.5 us (71%)
  starting transfers between devices  24.3 us (20%)
  waiting for transfers between devices  8.23 us (7%)
    pallas_call x3, Pallas kernels, main(): pl.pallas_call(functools.partial(main_kernel, low=low, n_ghost=n_ghost, n...  45.2 us
    pallas_call x1, Pallas kernels, place(): pl.pallas_call(place_kernel, out_shape=(shape((slots, C), BF16), shape((s...  21.2 us
    ppermute x2, starting transfers between devices, to_ring(): return lax.ppermute(rows, 'tile', ring)  13.7 us
    ppermute x2, waiting for transfers between devices, exchange(): lax.ppermute(far_rows, 'dom', far)  8.21 us
    pallas_call x1, Pallas kernels, body(): pl.pallas_call(radial_kernel, out_shape=(shape((tiles * TE, C), BF16), sh...  7.93 us
    ppermute x2, starting transfers between devices, exchange(): lax.ppermute(far_rows, 'dom', far)  5.31 us
    ppermute x4, starting transfers between devices, to_flip(): return lax.ppermute(rows, 'tile', flip)  4.9 us
    pallas_call x1, Pallas kernels, pick(): pl.pallas_call(functools.partial(pick_kernel, n=n), out_shape=(shape((n,...  3.93 us
  transfers between devices with their start and end apart: 11, of which 1 were waited for; matrix products, arithmetic and copies ran while one was open for 0% of the time, Pallas kernels for 62%

profile of v4, /device:TPU:10, one launch (start us, length us, event | category | flops | bytes accessed | tf_op | source)
XLA Modules:
  0.0 119.4 jit_solution(3718618394797841100)
XLA Ops:
  0.0 2.4 %mix.1.refs_1_ = bf16[1168,256]{1,0:T(8,128)(2,1)} custom-call(bf16[256,1152]{1,0:T(8,128)(2,1)} %x_ref.3, bf16[3,256,128]{2,1,0:T(8,128)(2,1)} %mix_ref.3, s32[1,256]{1,0:T(1,128)} %bitcast.3), custom_call_target="tpu_custom_call" | custom-call | flops 75497472 | bytes 2000000 | tf_op jit(solution)/shard_map/mix/pallas_call | solution.py:477
  2.4 1.6 %collective-permute-start = (bf16[1168,256]{1,0:T(8,128)(2,1)}, bf16[1168,256]{1,0:T(8,128)(2,1)}, u32[]{:S(2)}, u32[]{:S(2)}) collective-permute-start(bf16[1168,256]{1,0:T(8,128)(2,1)} %mix.1.refs_1_), channel_id=1, source_target_pairs={{0,2},{1,3},{2,4},{3,5},{4,6},{5,7},{6,0},{7,1},{8,10},{9,11},{10,... | collective-permute-start | bytes 1794056 | tf_op jit(solution)/shard_map/ppermute | solution.py:618
  4.0 2.8 %rank.1 = (s32[96,128]{1,0:T(8,128)}, s32[48,128]{1,0:T(8,128)}) custom-call(s32[1,8]{1,0:T(1,128)} %count_ref.5, s32[96,128]{1,0:T(8,128)} %bitcast.4), custom_call_target="tpu_custom_call" | custom-call | flops 4000000000 | bytes 1000000 | tf_op jit(solution)/shard_map/rank/pallas_call | solution.py:495
  6.7 1.5 %collective-permute-start.3 = (bf16[1168,256]{1,0:T(8,128)(2,1)}, bf16[1168,256]{1,0:T(8,128)(2,1)}, u32[]{:S(2)}, u32[]{:S(2)}) collective-permute-start(bf16[1168,256]{1,0:T(8,128)(2,1)} %mix.1.refs_1_), channel_id=1, source_target_pairs={{0,1},{1,0},{2,3},{3,2},{4,5},{5,4},{6,7},{7,6},{8,9},{9,8},{10,11... | collective-permute-start | bytes 1794056 | tf_op jit(solution)/shard_map/ppermute | solution.py:621
  8.2 7.9 %radial.1 = (bf16[12288,128]{1,0:T(8,128)(2,1)}, f32[256,128]{1,0:T(8,128)}) custom-call(s32[1,8]{1,0:T(1,128)} %count_ref.5, s32[96,128]{1,0:T(8,128)} %bitcast.6, bf16[12288,128]{1,0:T(8,128)(2,1)} %feat_ref.1, bf16[128,128]{1,0:T(8,128)(2,1)} %rin_ref.1), custom_call_target="tpu_custom_call" | custom-call | flops 10000000000 | bytes 6000000 | tf_op jit(solution)/shard_map/radial/pallas_call | solution.py:508
  16.2 0.0 collective-permute-start.2
  16.2 3.1 %base.1 = (f32[1152,256]{1,0:T(8,128)}, bf16[384,128]{1,0:T(8,128)(2,1)}) custom-call(f32[256,128]{1,0:T(8,128)} %get-tuple-element.33.rsum_ref, bf16[128,384]{1,0:T(8,128)(2,1)} %rout_ref.1, bf16[256,1152]{1,0:T(8,128)(2,1)} %x_ref.3, bf16[3,256,128]{2,1,0:T(8,128)(2,1)} %mix_ref.3), custom_call_target="tpu_custom_call" | custom-call | flops 1000000000 | bytes 2000000 | tf_op jit(solution)/shard_map/base/pallas_call | solution.py:562
  19.3 0.0 collective-permute-done.refs_3_
  19.3 1.3 %collective-permute-start.4 = (bf16[1168,256]{1,0:T(8,128)(2,1)}, bf16[1168,256]{1,0:T(8,128)(2,1)}, u32[]{:S(2)}, u32[]{:S(2)}) collective-permute-start(bf16[1168,256]{1,0:T(8,128)(2,1)} %collective-permute-done.refs_3_), channel_id=1, source_target_pairs={{0,1},{1,0},{2,3},{3,2},{4,5},{5,4},{6,7},{7,6},{8,9},{9,8},{10,11... | collective-permute-start | bytes 1794056 | tf_op jit(solution)/shard_map/ppermute | solution.py:621
  20.6 12.1 %collective-permute-start.1 = (bf16[1168,256]{1,0:T(8,128)(2,1)}, bf16[1168,256]{1,0:T(8,128)(2,1)}, u32[]{:S(2)}, u32[]{:S(2)}) collective-permute-start(bf16[1168,256]{1,0:T(8,128)(2,1)} %collective-permute-done.refs_3_), channel_id=1, source_target_pairs={{0,2},{1,3},{2,4},{3,5},{4,6},{5,7},{6,0},{7,1},{8,10},{9,11},{10,... | collective-permute-start | bytes 1794056 | tf_op jit(solution)/shard_map/ppermute | solution.py:618
  32.7 21.2 %place.1 = (bf16[16384,128]{1,0:T(8,128)(2,1)}, bf16[16384,128]{1,0:T(8,128)(2,1)}, s32[128,128]{1,0:T(8,128)}) custom-call(s32[1,8]{1,0:T(1,128)} %count_ref.5, s32[96,128]{1,0:T(8,128)} %get-tuple-element.37.pos_ref, s32[48,128]{1,0:T(8,128)} %get-tuple-element.31.span_ref.refs_0_, s32[96,128]{1,0:T(8,128)} %bitcast.5, s32[96,128]{1,0:T(8,128)} %bitcast.7, ...), custom_call_target="tpu_custom_call" | custom-call | flops 20000000000 | bytes 12000000 | tf_op jit(solution)/shard_map/place/pallas_call | solution.py:519
  53.9 0.0 collective-permute-done.2.refs_6_.refs_2_
  53.9 0.0 collective-permute-done.1.refs_5_.refs_0_
  53.9 0.1 collective-permute-start.5
  54.0 2.0 %collective-permute-start.6 = (bf16[1168,256]{1,0:T(8,128)(2,1)}, bf16[1168,256]{1,0:T(8,128)(2,1)}, u32[]{:S(2)}, u32[]{:S(2)}) collective-permute-start(bf16[1168,256]{1,0:T(8,128)(2,1)} %collective-permute-done.2.refs_6_.refs_2_), channel_id=1, source_target_pairs={{0,1},{1,0},{2,3},{3,2},{4,5},{5,4},{6,7},{7,6},{8,9},{9,8},{10,11... | collective-permute-start | bytes 1794056 | tf_op jit(solution)/shard_map/ppermute | solution.py:621
  56.0 0.0 collective-permute-done.3.refs_2_
  56.0 0.0 collective-permute-done.4.refs_4_
  56.0 17.9 %main_one.1 = (f32[1152,256]{1,0:T(8,128)}, bf16[4,1152,128]{2,1,0:T(8,128)(2,1)}, bf16[4,1152,128]{2,1,0:T(8,128)(2,1)}) custom-call(s32[48,128]{1,0:T(8,128)} %get-tuple-element.31.span_ref.refs_0_, bf16[1168,256]{1,0:T(8,128)(2,1)} %mix.1.refs_1_, bf16[1168,256]{1,0:T(8,128)(2,1)} %collective-permute-done.3.refs_2_, ...), custom_call_target="tpu_custom_call" | custom-call | flops 600000000 | bytes 600000 | tf_op jit(solution)/shard_map/main_one/pallas_call | solution.py:576
  74.0 0.1 collective-permute-start.9
  74.0 1.9 %collective-permute-start.10 = (bf16[4,1152,128]{2,1,0:T(8,128)(2,1)}, bf16[4,1152,128]{2,1,0:T(8,128)(2,1)}, u32[]{:S(2)}, u32[]{:S(2)}) collective-permute-start(bf16[4,1152,128]{2,1,0:T(8,128)(2,1)} %get-tuple-element.55), channel_id=1, source_target_pairs={{8,16},{16,8},{9,17},{17,9},{10,18},{18,10},{11,19},{19,11},{12,20... | collective-permute-start | bytes 3538952 | tf_op jit(solution)/shard_map/ppermute | solution.py:624
  76.0 0.0 collective-permute-done.5.refs_1_.refs_3_
  76.0 0.0 collective-permute-done.6.refs_3_.refs_4_
  76.0 3.9 %pick.1 = (bf16[4,1152,128]{2,1,0:T(8,128)(2,1)}, bf16[4,1152,128]{2,1,0:T(8,128)(2,1)}) custom-call(bf16[1168,256]{1,0:T(8,128)(2,1)} %collective-permute-done.1.refs_5_.refs_0_, bf16[1168,256]{1,0:T(8,128)(2,1)} %collective-permute-done.5.refs_1_.refs_3_, bf16[1168,256]{1,0:T(8,128)(2,1)} %collective-permute-done.2.refs_6_.refs_2_, ...), custom_call_target="tpu_custom_call" | custom-call | flops 200000000 | bytes 400000 | tf_op jit(solution)/shard_map/pick/pallas_call | solution.py:545
  79.9 0.3 collective-permute-start.7
  80.3 3.4 %collective-permute-start.8 = (bf16[4,1152,128]{2,1,0:T(8,128)(2,1)}, bf16[4,1152,128]{2,1,0:T(8,128)(2,1)}, u32[]{:S(2)}, u32[]{:S(2)}) collective-permute-start(bf16[4,1152,128]{2,1,0:T(8,128)(2,1)} %get-tuple-element.53), channel_id=1, source_target_pairs={{8,16},{16,8},{9,17},{17,9},{10,18},{18,10},{11,19},{19,11},{12,20... | collective-permute-start | bytes 3538952 | tf_op jit(solution)/shard_map/ppermute | solution.py:624
  83.7 0.0 collective-permute-done.9.refs_1_
  83.7 8.2 %collective-permute-done.10.refs_2_ = bf16[4,1152,128]{2,1,0:T(8,128)(2,1)} collective-permute-done((bf16[4,1152,128]{2,1,0:T(8,128)(2,1)}, bf16[4,1152,128]{2,1,0:T(8,128)(2,1)}, u32[]{:S(2)}, u32[]{:S(2)}) %collective-permute-start.10) | collective-permute-done | bytes 1179680 | tf_op jit(solution)/shard_map/ppermute | solution.py:624
  91.9 17.0 %main_two.1.refs_5_ = f32[1152,256]{1,0:T(8,128)} custom-call(s32[48,128]{1,0:T(8,128)} %get-tuple-element.31.span_ref.refs_0_, bf16[4,1152,128]{2,1,0:T(8,128)(2,1)} %collective-permute-done.9.refs_1_, bf16[4,1152,128]{2,1,0:T(8,128)(2,1)} %collective-permute-done.10.refs_2_, bf16[1168,256]{1,0:T(8,128)(2,1)} %collective-permute-done.5.refs_1_.refs_3_, ...), custom_call_target="tpu_custom_call" | custom-call | flops 600000000 | bytes 600000 | tf_op jit(solution)/shard_map/main_two/pallas_call | solution.py:576
  108.9 0.0 collective-permute-done.7.refs_1_
  108.9 0.0 collective-permute-done.8.refs_2_
  108.9 10.3 %main_three.1 = bf16[256,1152]{1,0:T(8,128)(2,1)} custom-call(s32[48,128]{1,0:T(8,128)} %get-tuple-element.31.span_ref.refs_0_, bf16[4,1152,128]{2,1,0:T(8,128)(2,1)} %collective-permute-done.7.refs_1_, bf16[4,1152,128]{2,1,0:T(8,128)(2,1)} %collective-permute-done.8.refs_2_, bf16[16384,128]{1,0:T(8,128)(2,1)} %get-tuple-element.43.refs_7_.refs_5_.refs_3_, ...), custom_call_target="tpu_custom_call" | custom-call | flops 400000000 | bytes 400000 | tf_op jit(solution)/shard_map/main_three/pallas_call | solution.py:576
Async XLA Ops:
  2.4 16.9 %collective-permute-start = (bf16[1168,256]{1,0:T(8,128)(2,1)}, bf16[1168,256]{1,0:T(8,128)(2,1)}, u32[]{:S(2)}, u32[]{:S(2)}) collective-permute-start(bf16[1168,256]{1,0:T(8,128)(2,1)} %mix.1.refs_1_), channel_id=1, source_target_pairs={{0,2},{1,3},{2,4},{3,5},{4,6},{5,7},{6,0},{7,1},{8,10},{9,11},{10,... | collective-permute-start | bytes 1794056 | tf_op jit(solution)/shard_map/ppermute | solution.py:618
  6.7 49.3 %collective-permute-start.3 = (bf16[1168,256]{1,0:T(8,128)(2,1)}, bf16[1168,256]{1,0:T(8,128)(2,1)}, u32[]{:S(2)}, u32[]{:S(2)}) collective-permute-start(bf16[1168,256]{1,0:T(8,128)(2,1)} %mix.1.refs_1_), channel_id=1, source_target_pairs={{0,1},{1,0},{2,3},{3,2},{4,5},{5,4},{6,7},{7,6},{8,9},{9,8},{10,11... | collective-permute-start | bytes 1794056 | tf_op jit(solution)/shard_map/ppermute | solution.py:621
  16.2 37.8 %collective-permute-start.2 = (bf16[1168,256]{1,0:T(8,128)(2,1)}, bf16[1168,256]{1,0:T(8,128)(2,1)}, u32[]{:S(2)}, u32[]{:S(2)}) collective-permute-start(bf16[1168,256]{1,0:T(8,128)(2,1)} %mix.1.refs_1_), channel_id=1, source_target_pairs={{2,0},{3,1},{4,2},{5,3},{6,4},{7,5},{0,6},{1,7},{10,8},{11,9},{12,... | collective-permute-start | bytes 1794056 | tf_op jit(solution)/shard_map/ppermute | solution.py:628
  19.3 36.7 %collective-permute-start.4 = (bf16[1168,256]{1,0:T(8,128)(2,1)}, bf16[1168,256]{1,0:T(8,128)(2,1)}, u32[]{:S(2)}, u32[]{:S(2)}) collective-permute-start(bf16[1168,256]{1,0:T(8,128)(2,1)} %collective-permute-done.refs_3_), channel_id=1, source_target_pairs={{0,1},{1,0},{2,3},{3,2},{4,5},{5,4},{6,7},{7,6},{8,9},{9,8},{10,11... | collective-permute-start | bytes 1794056 | tf_op jit(solution)/shard_map/ppermute | solution.py:621
  20.6 33.3 %collective-permute-start.1 = (bf16[1168,256]{1,0:T(8,128)(2,1)}, bf16[1168,256]{1,0:T(8,128)(2,1)}, u32[]{:S(2)}, u32[]{:S(2)}) collective-permute-start(bf16[1168,256]{1,0:T(8,128)(2,1)} %collective-permute-done.refs_3_), channel_id=1, source_target_pairs={{0,2},{1,3},{2,4},{3,5},{4,6},{5,7},{6,0},{7,1},{8,10},{9,11},{10,... | collective-permute-start | bytes 1794056 | tf_op jit(solution)/shard_map/ppermute | solution.py:618
  53.9 22.0 %collective-permute-start.5 = (bf16[1168,256]{1,0:T(8,128)(2,1)}, bf16[1168,256]{1,0:T(8,128)(2,1)}, u32[]{:S(2)}, u32[]{:S(2)}) collective-permute-start(bf16[1168,256]{1,0:T(8,128)(2,1)} %collective-permute-done.1.refs_5_.refs_0_), channel_id=1, source_target_pairs={{0,1},{1,0},{2,3},{3,2},{4,5},{5,4},{6,7},{7,6},{8,9},{9,8},{10,11... | collective-permute-start | bytes 1794056 | tf_op jit(solution)/shard_map/ppermute | solution.py:621
  54.0 22.0 %collective-permute-start.6 = (bf16[1168,256]{1,0:T(8,128)(2,1)}, bf16[1168,256]{1,0:T(8,128)(2,1)}, u32[]{:S(2)}, u32[]{:S(2)}) collective-permute-start(bf16[1168,256]{1,0:T(8,128)(2,1)} %collective-permute-done.2.refs_6_.refs_2_), channel_id=1, source_target_pairs={{0,1},{1,0},{2,3},{3,2},{4,5},{5,4},{6,7},{7,6},{8,9},{9,8},{10,11... | collective-permute-start | bytes 1794056 | tf_op jit(solution)/shard_map/ppermute | solution.py:621
  74.0 9.7 %collective-permute-start.9 = (bf16[4,1152,128]{2,1,0:T(8,128)(2,1)}, bf16[4,1152,128]{2,1,0:T(8,128)(2,1)}, u32[]{:S(2)}, u32[]{:S(2)}) collective-permute-start(bf16[4,1152,128]{2,1,0:T(8,128)(2,1)} %get-tuple-element.54), channel_id=1, source_target_pairs={{0,8},{8,0},{16,24},{24,16},{1,9},{9,1},{17,25},{25,17},{2,10},{10... | collective-permute-start | bytes 3538952 | tf_op jit(solution)/shard_map/ppermute | solution.py:624
  74.0 17.8 %collective-permute-start.10 = (bf16[4,1152,128]{2,1,0:T(8,128)(2,1)}, bf16[4,1152,128]{2,1,0:T(8,128)(2,1)}, u32[]{:S(2)}, u32[]{:S(2)}) collective-permute-start(bf16[4,1152,128]{2,1,0:T(8,128)(2,1)} %get-tuple-element.55), channel_id=1, source_target_pairs={{8,16},{16,8},{9,17},{17,9},{10,18},{18,10},{11,19},{19,11},{12,20... | collective-permute-start | bytes 3538952 | tf_op jit(solution)/shard_map/ppermute | solution.py:624
  79.9 29.0 %collective-permute-start.7 = (bf16[4,1152,128]{2,1,0:T(8,128)(2,1)}, bf16[4,1152,128]{2,1,0:T(8,128)(2,1)}, u32[]{:S(2)}, u32[]{:S(2)}) collective-permute-start(bf16[4,1152,128]{2,1,0:T(8,128)(2,1)} %get-tuple-element.52), channel_id=1, source_target_pairs={{0,8},{8,0},{16,24},{24,16},{1,9},{9,1},{17,25},{25,17},{2,10},{10... | collective-permute-start | bytes 3538952 | tf_op jit(solution)/shard_map/ppermute | solution.py:624
  80.3 28.7 %collective-permute-start.8 = (bf16[4,1152,128]{2,1,0:T(8,128)(2,1)}, bf16[4,1152,128]{2,1,0:T(8,128)(2,1)}, u32[]{:S(2)}, u32[]{:S(2)}) collective-permute-start(bf16[4,1152,128]{2,1,0:T(8,128)(2,1)} %get-tuple-element.53), channel_id=1, source_target_pairs={{8,16},{16,8},{9,17},{17,9},{10,18},{18,10},{11,19},{19,11},{12,20... | collective-permute-start | bytes 3538952 | tf_op jit(solution)/shard_map/ppermute | solution.py:624
